TPU v7x, 32 devices: a whole 2x2x4 slice. The times are simulated.
32 devices in a mesh: rows: 8 (over z, x), cols: 4 (over y, core).
Axes of the slice: x: 2, y: 2, z: 4, core: 2. Of those that a mesh axis runs over, the one named last changes fastest.
Arguments:
- panel_u: bfloat16 [8, 16, 1024, 256], P('rows', 'cols'), may hold values from -2.5 to 2.5
- panel_v: bfloat16 [8, 16, 1024, 256], P('rows', 'cols'), may hold values from -0.1875 to 0.1875
- panel_rank: int32 [8, 16], P('rows', 'cols'), may hold values from 128 to 256
- pivot_u: bfloat16 [2, 16, 1024, 256], P(None, 'cols', 'rows'), may hold values from -2.5 to 2.5
- pivot_v: bfloat16 [2, 16, 1024, 256], P(None, 'cols', 'rows'), may hold values from -0.1875 to 0.1875
- pivot_rank: int32 [2, 16], P(None, 'cols'), may hold values from 128 to 256
- orig_u: bfloat16 [2, 8, 1024, 256], P(None, 'rows'), may hold values from -6 to 6
- orig_v: bfloat16 [2, 8, 1024, 256], P(None, 'rows'), may hold values from -0.375 to 0.375
- sampler: bfloat16 [1024, 256], replicated, may hold values from -6 to 6
Outputs:
- basis: float32 [2, 8, 1024, 256], P(None, 'rows', 'cols')
- coeff: float32 [2, 8, 1024, 256], P(None, 'rows', 'cols')
Inputs may be any that keep to these rules, and one draw needn't show every extreme that they name: `panel_rank`: rank of each panel tile; factor columns at and beyond it carry no weight. `pivot_rank`: rank of each pivot row tile; factor columns at and beyond it carry no weight.
All inputs are finite; a program needn't handle non-finite values.
Results may differ from a plain program's by a relative error of at most 0.012.
Values may be sent and summed in bfloat16 or wider, within the bound.
No kernel may reach another device: no remote copies, remote signals or barrier semaphores. Data moves between devices by JAX's collectives and lax.ppermute only.
A program may use at most 64 MiB of HBM per device.

v0:
```python
import functools
import math

import jax
import jax.numpy as jnp
import numpy as np
from jax import lax
from jax.experimental import pallas as pl
from jax.experimental.pallas import tpu as pltpu
from jax.sharding import PartitionSpec as P

F32 = jnp.float32
BF16 = jnp.bfloat16
BLOCK = 32
GROUP = 4
SUB = 8
RING_MOST = 16
MIB = 1 << 20


def dot(a, b):
    return lax.dot_general(a, b, (((1,), (0,)), ((), ())), preferred_element_type=F32)


def dot00(a, b):
    return lax.dot_general(a, b, (((0,), (0,)), ((), ())), preferred_element_type=F32)


def dot11(a, b):
    return lax.dot_general(a, b, (((1,), (1,)), ((), ())), preferred_element_type=F32)


def split3(x):
    high = x.astype(BF16)
    rest = x - high.astype(F32)
    mid = rest.astype(BF16)
    low = (rest - mid.astype(F32)).astype(BF16)
    return high, mid, low


def reciprocal(x):
    guess = pl.reciprocal(x, approx=True)
    guess = guess * (2.0 - x * guess)
    return guess * (2.0 - x * guess)


def eliminate(panel, first):
    rows, width = panel.shape
    lanes = 128
    tile = (SUB, lanes)
    lane = lax.broadcasted_iota(jnp.int32, tile, 1)
    sub = lax.broadcasted_iota(jnp.int32, tile, 0)
    high = rows // SUB
    halves = width // lanes
    part = [
        [panel[v * SUB : (v + 1) * SUB, h * lanes : (h + 1) * lanes] for h in range(halves)]
        for v in range(high)
    ]
    mine = first // lanes
    pivots = [jnp.ones(tile, F32) for _ in range(high)]
    for k in range(0, rows, GROUP):
        at = first % lanes + k
        top, low = k // SUB, k % SUB
        inside = (lane >= at) & (lane < at + GROUP)
        column = [
            [jnp.broadcast_to(part[v][mine][:, at + m : at + m + 1], tile) for v in range(top, high)]
            for m in range(GROUP)
        ]
        small = [
            [jnp.broadcast_to(column[b][0][low + a : low + a + 1, :], tile) for b in range(a + 1)]
            for a in range(GROUP)
        ]
        row = []
        for a in range(GROUP):
            row.append([jnp.broadcast_to(part[top][h][low + a : low + a + 1, :], tile) for h in range(halves)])
            row[a][mine] = jnp.where(inside, jnp.where(lane == at + a, 1.0, 0.0), row[a][mine])
        factor = []
        for m in range(GROUP):
            inverse = reciprocal(small[m][m])
            pivots[top] = jnp.where(sub == low + m, small[m][m], pivots[top])
            for a in range(m + 1, GROUP):
                ratio = small[a][m] * inverse
                for b in range(m + 1, a + 1):
                    small[a][b] = small[a][b] - ratio * small[b][m]
                row[a] = [x - ratio * y for x, y in zip(row[a], row[m])]
            factor.append([c * inverse for c in column[m]])
            for b in range(m + 1, GROUP):
                column[b] = [c - f * small[b][m] for c, f in zip(column[b], factor[m])]
        for v in range(top, high):
            for h in range(halves):
                old = part[v][h]
                value = jnp.where(inside, 0.0, old) if h == mine else old
                for m in range(GROUP):
                    value = value - factor[m][v - top] * row[m][h]
                if v == top:
                    if low > 0:
                        value = jnp.where(sub < low, old, value)
                    for m in range(GROUP):
                        value = jnp.where(sub == low + m, row[m][h], value)
                part[v][h] = value
    done = []
    for v in range(high):
        scale = lax.rsqrt(pivots[v])
        cells = []
        for h in range(halves):
            value = part[v][h] * scale
            if h == mine:
                start = first % lanes
                value = jnp.where((lane > start + v * SUB + sub) & (lane < start + rows), 0.0, value)
            cells.append(value)
        done.append(jnp.concatenate(cells, 1))
    return jnp.concatenate(done, 0)


def invert_blocks(work, begin, end):
    width = work.shape[0]
    lane = lax.broadcasted_iota(jnp.int32, (1, width), 1)
    for first in range(begin, end, BLOCK):
        last = first + BLOCK
        panel = eliminate(work[first:last, :], first)
        work[first:last, :] = panel
        if last < width:
            base = last // 128 * 128
            high, mid, low = split3(panel)
            left = jnp.concatenate([high, high, mid, mid, high, low], 0)[:, base:]
            right = jnp.concatenate([high, mid, high, mid, low, high], 0)
            update = dot00(left, right)[last - base :, :]
            inside = (lane >= first) & (lane < last)
            work[last:, :] = jnp.where(inside, 0.0, work[last:, :]) - update


def gram_of(info, mine, other, yt, work):
    half = mine.shape[1]
    core = info[0]
    yt[:, pl.ds(pl.multiple_of(core * half, 128), half)] = mine[...]
    yt[:, pl.ds(pl.multiple_of((1 - core) * half, 128), half)] = other[...]
    high, mid, low = split3(yt[...])
    cross = dot11(high, mid) + dot11(high, low)
    work[...] = dot11(high, high) + (cross + cross.T + dot11(mid, mid))


def apply_factor(info, y, work, qt, basis, q):
    width, order = y.shape
    row = lax.broadcasted_iota(jnp.int32, (width, width), 0)
    col = lax.broadcasted_iota(jnp.int32, (width, width), 1)
    m_high, m_low, _ = split3(jnp.where(col <= row, work[...], 0.0))
    high, mid, _ = split3(y[...])
    product = dot(m_high, high) + (dot(m_high, mid) + dot(m_low, high))
    qt[...] = product.astype(BF16)
    q[...] = product
    share = basis.shape[0]
    rows = q[:, pl.ds(pl.multiple_of(info[1] * share, 128), share)]
    basis[...] = rows.T * math.sqrt(order)


def orthonormal_kernel(info, mine, other, qt, basis, yt, work):
    gram_of(info, mine, other, yt, work)
    invert_blocks(work, 0, work.shape[0])
    apply_factor(info, yt, work, qt, basis, yt)


def first_kernel(info, mine, other, yt, out, work):
    gram_of(info, mine, other, yt, work)
    invert_blocks(work, 0, work.shape[0] // 2)
    out[...] = work[...]


def last_kernel(info, y, begun, qt, basis, q, work):
    work[...] = begun[...]
    invert_blocks(work, work.shape[0] // 2, work.shape[0])
    apply_factor(info, y, work, qt, basis, q)


def fetch(blocks, buffer, sems, which):
    slab = blocks[0].shape[1]
    return [
        [
            pltpu.make_async_copy(b.at[j], buffer.at[j, pl.ds(n * slab, slab)], sems.at[which, j, n])
            for n, b in enumerate(blocks)
        ]
        for j in range(buffer.shape[0])
    ]


def update_kernel(blocks, info, ranks, panel_vt, sampler_t, panel_u, *refs):
    u, v = refs[:blocks], refs[blocks : 2 * blocks]
    cross, give, keep, u_buf, v_buf, sems = refs[2 * blocks :]
    priors, order, width = u_buf.shape
    slab = order // blocks
    half = keep.shape[1]
    core = info[0]
    copies = [fetch(u, u_buf, sems, 0), fetch(v, v_buf, sems, 1)]
    for j in range(priors):
        for t in range(2):
            for copy in copies[t][j]:
                copy.start()
    spans = [pl.ds(pl.multiple_of(info[2 + b] * slab, 128), slab) for b in range(blocks)]
    row = lax.broadcasted_iota(jnp.int32, (width, width), 0)
    col = lax.broadcasted_iota(jnp.int32, (width, width), 1)
    drawn = jnp.concatenate([sampler_t[:, span] for span in spans], 1)
    terms = []
    for j in range(priors):
        for t in range(2):
            for copy in copies[t][j]:
                copy.wait()
        sampled = dot(drawn, u_buf[j])
        met = dot(jnp.concatenate([panel_vt[j, :, span] for span in spans], 1), v_buf[j])
        met = jnp.where((row < ranks[0, j]) & (col < ranks[1, j]), met, 0.0).astype(BF16)
        cross[j] = met
        terms.append(dot11(sampled.astype(BF16), met).astype(BF16))
    for out, which in ((give, 1 - core), (keep, core)):
        rows = pl.ds(pl.multiple_of(which * half, 128), half)
        total = jnp.zeros((width, half), F32)
        for j in range(priors):
            total += dot11(terms[j], panel_u[j, rows, :])
        out[...] = total.astype(out.dtype)


def project_kernel(blocks, info, qt, panel_u, cross, *refs):
    u = refs[:blocks]
    give, keep, work, u_buf, sems = refs[blocks:]
    priors, order, width = u_buf.shape
    slab = order // blocks
    pairs, share, _ = keep.shape
    core = info[0]
    copies = fetch(u, u_buf, sems, 0)
    for each in copies:
        for copy in each:
            copy.start()
    mids = []
    for j in range(priors):
        inner = dot(qt[...], panel_u[j]).astype(BF16)
        mids.append(dot(inner, cross[j]).astype(BF16))
    for each in copies:
        for copy in each:
            copy.wait()
    some = max(1, blocks // 2)
    for begin in range(0, blocks, some):
        total = jnp.zeros((some * slab, width), F32)
        for j in range(priors):
            total += dot11(u_buf[j, begin * slab : (begin + some) * slab, :], mids[j])
        for n in range(some):
            rows = pl.ds(pl.multiple_of(info[2 + begin + n] * slab, SUB), slab)
            work[rows, :] = total[n * slab : (n + 1) * slab, :]
    for a in range(pairs):
        for out, which in ((give, 1 - core), (keep, core)):
            rows = pl.ds(pl.multiple_of((2 * a + which) * share, SUB), share)
            out[a] = work[rows, :].astype(out.dtype)


def left_kernel(info, qt, orig_u, orig_v, out):
    share = out.shape[0]
    left = dot(qt[...], orig_u[...]).astype(BF16)
    rows = orig_v[pl.ds(pl.multiple_of(info[1] * share, SUB), share), :]
    out[...] = dot11(rows, left)


def turn_kernel(panel_v, sampler, panel_vt, sampler_t):
    sampler_t[...] = sampler[...].T
    for j in range(panel_v.shape[0]):
        panel_vt[j] = panel_v[j].T


def start_kernel(info, sampler_t, orig_u, orig_v, out):
    half = out.shape[2]
    for c in range(out.shape[0]):
        proj = dot(sampler_t[...], orig_v[c]).astype(BF16)
        rows = pl.ds(pl.multiple_of(info[0] * half, SUB), half)
        out[c] = dot11(proj, orig_u[c, rows, :])


def run(kernel, scalars, arrays, outs, scratch, limit, flops, name, apart=()):
    smem = pl.BlockSpec(memory_space=pltpu.SMEM)
    vmem = pl.BlockSpec(memory_space=pltpu.VMEM)
    shapes = [jax.ShapeDtypeStruct(*o) for o in outs]
    moved = sum(a.size * a.dtype.itemsize for a in list(arrays) + list(apart) + shapes)
    return pl.pallas_call(
        kernel,
        out_shape=shapes,
        in_specs=[smem] * len(scalars) + [vmem] * len(arrays) + [pl.BlockSpec(memory_space=pl.ANY)] * len(apart),
        out_specs=[vmem] * len(shapes),
        scratch_shapes=scratch,
        compiler_params=pltpu.CompilerParams(vmem_limit_bytes=limit * MIB),
        cost_estimate=pl.CostEstimate(flops=flops, bytes_accessed=moved, transcendentals=0),
        name=name,
    )(*scalars, *arrays, *apart)


def ring_order(count):
    if count % 2:
        return list(range(count))
    return list(range(0, count, 2)) + list(range(count - 1, 0, -2))


class Ring:
    def __init__(self, arrays, order, axis):
        count = len(order)
        self.count, self.axis, self.near = count, axis, (count - 1) // 2
        self.ahead = [(order[(p + 1) % count], order[p]) for p in range(count)]
        self.behind = [(order[p], order[(p + 1) % count]) for p in range(count)]
        self.found = [{0: a} for a in arrays]
        self.up, self.down = list(arrays), list(arrays)

    def step(self, number):
        for t in range(2):
            if number <= self.near or t == 0:
                self.up[t] = lax.ppermute(self.up[t], self.axis, self.ahead)
                self.found[t][number] = self.up[t]
            if number <= self.near or t == 1:
                self.down[t] = lax.ppermute(self.down[t], self.axis, self.behind)
                self.found[t][self.count - number] = self.down[t]

    def hold(self, value, t, number):
        if number > self.near:
            return value
        places = (number, self.count - number)
        value, *kept = lax.optimization_barrier((value, *(self.found[t][d] for d in places)))
        for d, block in zip(places, kept):
            self.found[t][d] = block
        return value

    def tie(self, value, number, which=(0, 1)):
        lists = [(self.up, t, number) for t in which if number <= self.near or t == 0]
        lists += [(self.down, t, self.count - number) for t in which if number <= self.near or t == 1]
        value, *held = lax.optimization_barrier((value, *(way[t] for way, t, _ in lists)))
        for (way, t, place), block in zip(lists, held):
            way[t] = self.found[t][place] = block
        return value

    def blocks(self, t):
        return [self.found[t][d] for d in range(self.count)]


def body(panel_u, panel_v, panel_rank, pivot_u, pivot_v, pivot_rank, orig_u, orig_v, sampler):
    order, width = panel_u.shape[2:]
    priors = panel_u.shape[1]
    pivots = pivot_u.shape[0]
    count = lax.axis_size("rows")
    cols = lax.axis_size("cols")
    pairs = cols // 2
    half, share = order // 2, order // cols
    me = lax.axis_index("cols")
    core, pair = me % 2, me // 2
    swap = [(i, i ^ 1) for i in range(cols)]

    ring = ring_order(count)
    place = np.argsort(np.array(ring))
    table = np.array([[ring[(place[r] + d) % count] for d in range(count)] for r in range(count)], np.int32)
    if count > RING_MOST:
        table = np.zeros((count, 1), np.int32)
    sources = jnp.asarray(table)[lax.axis_index("rows")]
    info = jnp.concatenate([jnp.stack([core, me]).astype(jnp.int32), sources])

    panel_u, panel_v, orig_u, orig_v = panel_u[0], panel_v[0], orig_u[:, 0], orig_v[:, 0]
    square = 2 * width * width
    panel_vt, sampler_t = run(
        turn_kernel, [], [panel_v, sampler], [((priors, width, order), BF16), ((sampler.shape[1], order), BF16)], [], 12,
        10 * square * order, "turn"
    )
    whole = count > RING_MOST
    if not whole:
        now = Ring([pivot_u[0], pivot_v[0]], ring, "rows")
        now.step(1)
        panel_vt = now.tie(panel_vt, 1, (1,))
        now.step(2)
    (start,) = run(
        start_kernel, [info], [sampler_t, orig_u, orig_v], [((pivots, width, half), F32)], [], 12,
        pivots * square * (order + half), "start"
    )
    if not whole:
        start = now.tie(start, 2, (1,))
        for number in range(3, count // 2 + 1):
            now.step(number)

    def shifted(x, shift):
        return lax.ppermute(x, "cols", [(i, (i + 2 * shift) % cols) for i in range(cols)])

    buffer = pltpu.VMEM((priors, order, width), BF16)
    matrix = pltpu.VMEM((width, width), F32)
    tall = pltpu.VMEM((width, order), F32)

    def updated(c, blocks_u, blocks_v):
        blocks = len(blocks_u)
        ranks = jnp.stack([panel_rank[0], pivot_rank[c]])
        return run(
            functools.partial(update_kernel, blocks), [info, ranks], [panel_vt, sampler_t, panel_u],
            [((priors, width, width), BF16), ((width, half), BF16), ((width, half), F32)],
            [buffer, buffer, pltpu.SemaphoreType.DMA((2, priors, blocks))], 20,
            3 * priors * square * (3 * order + width), "update", (*blocks_u, *blocks_v)
        )

    def finished(c, blocks_u, cross, give, keep, beside):
        blocks = len(blocks_u)
        chip = keep + lax.ppermute(give, "cols", swap).astype(F32)
        sent = chip.astype(BF16)
        for shift in range(1, pairs):
            chip = chip + shifted(sent, shift).astype(F32)
        if beside is not None:
            chip = beside.tie(chip, 2)
            beside.step(3)
        ymine = start[c] - chip
        yother = lax.ppermute(ymine, "cols", swap)
        finals = [((width, order), BF16), ((share, width), F32)]
        if beside is None:
            qt, rows = run(
                orthonormal_kernel, [info], [ymine, yother], finals, [tall, matrix], 12, 128 * square * order, "orthonormal"
            )
        else:
            yt, work = run(
                first_kernel, [info], [ymine, yother], [((width, order), F32), ((width, width), F32)], [matrix], 12,
                64 * square * order, "orthonormal_first"
            )
            work = beside.tie(work, 3)
            beside.step(4)
            qt, rows = run(
                last_kernel, [info], [yt, work], finals, [tall, matrix], 12, 64 * square * order, "orthonormal_last"
            )
            beside.found[0][0], qt = lax.optimization_barrier((beside.found[0][0], qt))
        give, keep = run(
            functools.partial(project_kernel, blocks), [info], [qt, panel_u, cross],
            [((pairs, share, width), BF16), ((pairs, share, width), F32)],
            [pltpu.VMEM((order, width), F32), buffer, pltpu.SemaphoreType.DMA((1, priors, blocks))], 16,
            3 * priors * square * (2 * order + width), "project", blocks_u
        )
        (own,) = run(
            left_kernel, [info], [qt, orig_u[c], orig_v[c]], [((share, width), F32)], [], 8,
            square * (order + share), "left"
        )
        chip = keep + lax.ppermute(give, "cols", swap).astype(F32)
        total = lax.dynamic_index_in_dim(chip, pair, 0, False)
        for shift in range(1, pairs):
            sent = lax.dynamic_index_in_dim(chip, (pair + shift) % pairs, 0, False).astype(BF16)
            total = total + shifted(sent, shift).astype(F32)
        return rows, own - total

    results = []
    if whole:
        for c in range(pivots):
            blocks_u, blocks_v = ([lax.all_gather(x[c], "rows", axis=1, tiled=True)] for x in (pivot_u, pivot_v))
            results.append(finished(c, blocks_u, *updated(c, blocks_u, blocks_v), None))
    else:
        for c in range(pivots):
            later = None
            if c + 1 < pivots:
                later = Ring([now.hold(pivot_u[c + 1], 0, now.near), now.hold(pivot_v[c + 1], 1, now.near)], ring, "rows")
                later.step(1)
            cross, give, keep = updated(c, now.blocks(0), now.blocks(1))
            if later is not None:
                give = later.tie(give, 1)
                later.step(2)
            results.append(finished(c, now.blocks(0), cross, give, keep, later))
            now = later
    basis, coeff = zip(*results)
    return (jnp.stack(basis)[:, None], jnp.stack(coeff)[:, None])


def solution(mesh):
    placed = (
        P("rows", "cols", None, None),
        P("rows", "cols", None, None),
        P("rows", "cols"),
        P(None, "cols", "rows", None),
        P(None, "cols", "rows", None),
        P(None, "cols"),
        P(None, "rows", None, None),
        P(None, "rows", None, None),
        P(),
    )
    return jax.shard_map(
        body,
        mesh=mesh,
        in_specs=placed,
        out_specs=(P(None, "rows", "cols", None), P(None, "rows", "cols", None)),
        check_vma=False,
    )
```

profile of v0, /device:TPU:0, one launch (start us, length us, event | category | flops | bytes accessed | tf_op | source)
XLA Modules:
  0.0 167.9 jit_solution(8308385576506975777)
XLA Ops:
  1.7 3.0 %collective-permute-start = (bf16[4,128,256]{2,1,0:T(8,128)(2,1)S(1)}, bf16[4,128,256]{2,1,0:T(8,128)(2,1)}, u32[]{:S(2)}, u32[]{:S(2)}) collective-permute-start(bf16[4,128,256]{2,1,0:T(8,128)(2,1)S(1)} %get-tuple-element.103.refs_8_), channel_id=1, source_target_pairs={{8,0},{16,8},{24,16},{28,24},{20,28},{12,20},{4,12},{0,4},{9,1},{1... | collective-permute-start | bytes 786440 | tf_op jit(solution)/shard_map/ppermute | solution.py:307
  5.9 1.9 %collective-permute-start.4 = (bf16[4,128,256]{2,1,0:T(8,128)(2,1)S(1)}, bf16[4,128,256]{2,1,0:T(8,128)(2,1)S(1)}, u32[]{:S(2)}, u32[]{:S(2)}) collective-permute-start(bf16[4,128,256]{2,1,0:T(8,128)(2,1)S(1)} %get-tuple-element.104.refs_0_), channel_id=1, source_target_pairs={{8,0},{16,8},{24,16},{28,24},{20,28},{12,20},{4,12},{0,4},{9,1},{1... | collective-permute-start | bytes 786440 | tf_op jit(solution)/shard_map/ppermute | solution.py:307
  8.0 1.6 copy-done.13
  12.0 2.0 %collective-permute-done.1.refs_15_ = bf16[4,128,256]{2,1,0:T(8,128)(2,1)} collective-permute-done((bf16[4,128,256]{2,1,0:T(8,128)(2,1)S(1)}, bf16[4,128,256]{2,1,0:T(8,128)(2,1)}, u32[]{:S(2)}, u32[]{:S(2)}) %collective-permute-start.1) | collective-permute-done | bytes 262176 | tf_op jit(solution)/shard_map/ppermute | solution.py:310
  17.5 2.0 %collective-permute-start.5 = (bf16[4,128,256]{2,1,0:T(8,128)(2,1)S(1)}, bf16[4,128,256]{2,1,0:T(8,128)(2,1)S(1)}, u32[]{:S(2)}, u32[]{:S(2)}) collective-permute-start(bf16[4,128,256]{2,1,0:T(8,128)(2,1)S(1)} %collective-permute-done.4.refs_1_), channel_id=1, source_target_pairs={{8,0},{16,8},{24,16},{28,24},{20,28},{12,20},{4,12},{0,4},{9,1},{1... | collective-permute-start | bytes 786440 | tf_op jit(solution)/shard_map/ppermute | solution.py:307
  20.3 1.6 start.1
  25.2 2.7 %collective-permute-done.5.refs_2_ = bf16[4,128,256]{2,1,0:T(8,128)(2,1)S(1)} collective-permute-done((bf16[4,128,256]{2,1,0:T(8,128)(2,1)S(1)}, bf16[4,128,256]{2,1,0:T(8,128)(2,1)S(1)}, u32[]{:S(2)}, u32[]{:S(2)}) %collective-permute-start.5) | collective-permute-done | bytes 262176 | tf_op jit(solution)/shard_map/ppermute | solution.py:307
  27.9 1.7 collective-permute-start.6
  31.6 5.4 %collective-permute-done.12.refs_13_ = bf16[4,128,256]{2,1,0:T(8,128)(2,1)S(1)} collective-permute-done((bf16[4,128,256]{2,1,0:T(8,128)(2,1)S(1)}, bf16[4,128,256]{2,1,0:T(8,128)(2,1)S(1)}, u32[]{:S(2)}, u32[]{:S(2)}) %collective-permute-start.12) | collective-permute-done | bytes 262176 | tf_op jit(solution)/shard_map/ppermute | solution.py:310
  37.2 1.9 %collective-permute-start.10 = (bf16[4,128,256]{2,1,0:T(8,128)(2,1)S(1)}, bf16[4,128,256]{2,1,0:T(8,128)(2,1)S(1)}, u32[]{:S(2)}, u32[]{:S(2)}) collective-permute-start(bf16[4,128,256]{2,1,0:T(8,128)(2,1)S(1)} %collective-permute-done.6.refs_3_), channel_id=1, source_target_pairs={{8,0},{16,8},{24,16},{28,24},{20,28},{12,20},{4,12},{0,4},{9,1},{1... | collective-permute-start | bytes 786440 | tf_op jit(solution)/shard_map/ppermute | solution.py:307
  39.1 3.7 %collective-permute-done.11.refs_11_ = bf16[4,128,256]{2,1,0:T(8,128)(2,1)S(1)} collective-permute-done((bf16[4,128,256]{2,1,0:T(8,128)(2,1)S(1)}, bf16[4,128,256]{2,1,0:T(8,128)(2,1)S(1)}, u32[]{:S(2)}, u32[]{:S(2)}) %collective-permute-start.11) | collective-permute-done | bytes 262176 | tf_op jit(solution)/shard_map/ppermute | solution.py:307
  42.8 1.7 collective-permute-start.15
  44.8 1.7 collective-permute-start.14
  46.5 1.8 %collective-permute-done.13.refs_12_ = bf16[4,128,256]{2,1,0:T(8,128)(2,1)S(1)} collective-permute-done((bf16[4,128,256]{2,1,0:T(8,128)(2,1)S(1)}, bf16[4,128,256]{2,1,0:T(8,128)(2,1)S(1)}, u32[]{:S(2)}, u32[]{:S(2)}) %collective-permute-start.13) | collective-permute-done | bytes 262176 | tf_op jit(solution)/shard_map/ppermute | solution.py:310
  48.4 9.1 %update.2 = (bf16[4,256,256]{2,1,0:T(8,128)(2,1)S(1)}, bf16[256,512]{1,0:T(8,128)(2,1)S(1)}, f32[256,512]{1,0:T(8,128)S(1)}) custom-call(s32[10]{0:T(128)S(1)} %pad_add_fusion.2.info, s32[2,4]{1,0:T(2,128)S(1)} %get-tuple-element.108.ranks, bf16[4,256,1024]{2,1,0:T(8,128)(2,1)S(1)} %get-tuple-element.54.panel_vt, ...), custom_call_target="tpu_custom_call" | custom-call | flops 5234491392 | bytes 10223616 | tf_op jit(solution)/shard_map/update/pallas_call | solution.py:277
  59.3 2.0 %collective-permute-start.19 = (bf16[256,512]{1,0:T(8,128)(2,1)S(1)}, bf16[256,512]{1,0:T(8,128)(2,1)S(1)}, u32[]{:S(2)}, u32[]{:S(2)}) collective-permute-start(bf16[256,512]{1,0:T(8,128)(2,1)S(1)} %fusion), channel_id=1, source_target_pairs={{0,2},{1,3},{2,0},{3,1},{4,6},{5,7},{6,4},{7,5},{8,10},{9,11},{10,... | collective-permute-start | bytes 786440 | tf_op jit(solution)/shard_map/ppermute | solution.py:376
  65.3 2.6 %collective-permute-done.19 = bf16[256,512]{1,0:T(8,128)(2,1)S(1)} collective-permute-done((bf16[256,512]{1,0:T(8,128)(2,1)S(1)}, bf16[256,512]{1,0:T(8,128)(2,1)S(1)}, u32[]{:S(2)}, u32[]{:S(2)}) %collective-permute-start.19) | collective-permute-done | bytes 262176 | tf_op jit(solution)/shard_map/ppermute | solution.py:376
  68.0 2.5 %collective-permute-done.20.refs_2_ = bf16[4,128,256]{2,1,0:T(8,128)(2,1)S(1)} collective-permute-done((bf16[4,128,256]{2,1,0:T(8,128)(2,1)S(1)}, bf16[4,128,256]{2,1,0:T(8,128)(2,1)S(1)}, u32[]{:S(2)}, u32[]{:S(2)}) %collective-permute-start.20) | collective-permute-done | bytes 262176 | tf_op jit(solution)/shard_map/ppermute | solution.py:307
  70.4 4.5 %collective-permute-done.21.refs_10_ = bf16[4,128,256]{2,1,0:T(8,128)(2,1)S(1)} collective-permute-done((bf16[4,128,256]{2,1,0:T(8,128)(2,1)S(1)}, bf16[4,128,256]{2,1,0:T(8,128)(2,1)S(1)}, u32[]{:S(2)}, u32[]{:S(2)}) %collective-permute-start.21) | collective-permute-done | bytes 262176 | tf_op jit(solution)/shard_map/ppermute | solution.py:307
  74.9 2.5 %collective-permute-done.23.refs_14_ = bf16[4,128,256]{2,1,0:T(8,128)(2,1)S(1)} collective-permute-done((bf16[4,128,256]{2,1,0:T(8,128)(2,1)S(1)}, bf16[4,128,256]{2,1,0:T(8,128)(2,1)S(1)}, u32[]{:S(2)}, u32[]{:S(2)}) %collective-permute-start.23) | collective-permute-done | bytes 262176 | tf_op jit(solution)/shard_map/ppermute | solution.py:310
  77.6 1.6 collective-permute-start.25
  79.3 1.6 collective-permute-start.26
  81.8 7.9 %orthonormal_first.1 = (f32[256,1024]{1,0:T(8,128)S(1)}, f32[256,256]{1,0:T(8,128)S(1)}) custom-call(s32[10]{0:T(128)S(1)} %pad_add_fusion.2.info, f32[256,512]{1,0:T(8,128)S(1)} %bitcast_subtract_fusion.1.mine, f32[256,512]{1,0:T(8,128)S(1)} %collective-permute-done.24.other), custom_call_target="tpu_custom_call" | custom-call | flops 8589934592 | bytes 2359296 | tf_op jit(solution)/shard_map/orthonormal_first/pallas_call | solution.py:277
  89.7 2.3 %collective-permute-done.26.refs_11_ = bf16[4,128,256]{2,1,0:T(8,128)(2,1)S(1)} collective-permute-done((bf16[4,128,256]{2,1,0:T(8,128)(2,1)S(1)}, bf16[4,128,256]{2,1,0:T(8,128)(2,1)S(1)}, u32[]{:S(2)}, u32[]{:S(2)}) %collective-permute-start.26) | collective-permute-done | bytes 262176 | tf_op jit(solution)/shard_map/ppermute | solution.py:307
  92.0 2.6 %collective-permute-done.28.refs_13_ = bf16[4,128,256]{2,1,0:T(8,128)(2,1)S(1)} collective-permute-done((bf16[4,128,256]{2,1,0:T(8,128)(2,1)S(1)}, bf16[4,128,256]{2,1,0:T(8,128)(2,1)S(1)}, u32[]{:S(2)}, u32[]{:S(2)}) %collective-permute-start.28) | collective-permute-done | bytes 262176 | tf_op jit(solution)/shard_map/ppermute | solution.py:310
  96.6 7.5 %orthonormal_last.1 = (bf16[256,1024]{1,0:T(8,128)(2,1)S(1)}, f32[256,256]{1,0:T(8,128)S(1)}) custom-call(s32[10]{0:T(128)S(1)} %pad_add_fusion.2.info, f32[256,1024]{1,0:T(8,128)S(1)} %get-tuple-element.71.y, f32[256,256]{1,0:T(8,128)S(1)} %get-tuple-element.77.begun), custom_call_target="tpu_custom_call" | custom-call | flops 8589934592 | bytes 2097152 | tf_op jit(solution)/shard_map/orthonormal_last/pallas_call | solution.py:277
  104.9 10.1 %update.3 = (bf16[4,256,256]{2,1,0:T(8,128)(2,1)S(1)}, bf16[256,512]{1,0:T(8,128)(2,1)S(1)}, f32[256,512]{1,0:T(8,128)S(1)}) custom-call(s32[10]{0:T(128)S(1)} %pad_add_fusion.2.info, s32[2,4]{1,0:T(2,128)S(1)} %get-tuple-element.109.ranks, bf16[4,256,1024]{2,1,0:T(8,128)(2,1)S(1)} %get-tuple-element.54.panel_vt, ...), custom_call_target="tpu_custom_call" | custom-call | flops 5234491392 | bytes 10223616 | tf_op jit(solution)/shard_map/update/pallas_call | solution.py:277
  117.3 7.0 %project.2 = (bf16[2,256,256]{2,1,0:T(8,128)(2,1)}, f32[2,256,256]{2,1,0:T(8,128)S(1)}) custom-call(s32[10]{0:T(128)S(1)} %pad_add_fusion.2.info, bf16[256,1024]{1,0:T(8,128)(2,1)S(1)} %get-tuple-element.88.qt, bf16[4,1024,256]{2,1,0:T(8,128)(2,1)S(1)} %bitcast.65, bf16[4,256,256]{2,1,0:T(8,128)(2,1)S(1)} %get-tuple-element.89.cross, ...), custom_call_target="tpu_custom_call" | custom-call | flops 3623878656 | bytes 6029312 | tf_op jit(solution)/shard_map/project/pallas_call | solution.py:277
  128.1 1.6 collective-permute-start.35
  129.7 15.3 %orthonormal.1 = (bf16[256,1024]{1,0:T(8,128)(2,1)S(1)}, f32[256,256]{1,0:T(8,128)S(1)}) custom-call(s32[10]{0:T(128)S(1)} %pad_add_fusion.2.info, f32[256,512]{1,0:T(8,128)S(1)} %bitcast_subtract_fusion.mine, f32[256,512]{1,0:T(8,128)} %collective-permute-done.33.other), custom_call_target="tpu_custom_call" | custom-call | flops 17179869184 | bytes 1835008 | tf_op jit(solution)/shard_map/orthonormal/pallas_call | solution.py:277
  145.8 6.8 %project.3 = (bf16[2,256,256]{2,1,0:T(8,128)(2,1)}, f32[2,256,256]{2,1,0:T(8,128)S(1)}) custom-call(s32[10]{0:T(128)S(1)} %pad_add_fusion.2.info, bf16[256,1024]{1,0:T(8,128)(2,1)S(1)} %get-tuple-element.92.qt, bf16[4,1024,256]{2,1,0:T(8,128)(2,1)S(1)} %bitcast.66, bf16[4,256,256]{2,1,0:T(8,128)(2,1)S(1)} %copy-done.34, ...), custom_call_target="tpu_custom_call" | custom-call | flops 3623878656 | bytes 6029312 | tf_op jit(solution)/shard_map/project/pallas_call | solution.py:277
  163.8 3.2 %collective-permute-done.37 = bf16[256,256]{1,0:T(8,128)(2,1)S(1)} collective-permute-done((bf16[256,256]{1,0:T(8,128)(2,1)S(1)}, bf16[256,256]{1,0:T(8,128)(2,1)S(1)}, u32[]{:S(2)}, u32[]{:S(2)}) %collective-permute-start.37) | collective-permute-done | bytes 131104 | tf_op jit(solution)/shard_map/ppermute | solution.py:376
  (151 shorter events, 43.4 us)
Async XLA Ops:
  1.7 10.3 %collective-permute-start = (bf16[4,128,256]{2,1,0:T(8,128)(2,1)S(1)}, bf16[4,128,256]{2,1,0:T(8,128)(2,1)}, u32[]{:S(2)}, u32[]{:S(2)}) collective-permute-start(bf16[4,128,256]{2,1,0:T(8,128)(2,1)S(1)} %get-tuple-element.103.refs_8_), channel_id=1, source_target_pairs={{8,0},{16,8},{24,16},{28,24},{20,28},{12,20},{4,12},{0,4},{9,1},{1... | collective-permute-start | bytes 786440 | tf_op jit(solution)/shard_map/ppermute | solution.py:307
  4.7 9.3 %collective-permute-start.1 = (bf16[4,128,256]{2,1,0:T(8,128)(2,1)S(1)}, bf16[4,128,256]{2,1,0:T(8,128)(2,1)}, u32[]{:S(2)}, u32[]{:S(2)}) collective-permute-start(bf16[4,128,256]{2,1,0:T(8,128)(2,1)S(1)} %get-tuple-element.103.refs_8_), channel_id=1, source_target_pairs={{0,8},{8,16},{16,24},{24,28},{28,20},{20,12},{12,4},{4,0},{1,9},{9... | collective-permute-start | bytes 786440 | tf_op jit(solution)/shard_map/ppermute | solution.py:310
  5.9 11.6 %collective-permute-start.4 = (bf16[4,128,256]{2,1,0:T(8,128)(2,1)S(1)}, bf16[4,128,256]{2,1,0:T(8,128)(2,1)S(1)}, u32[]{:S(2)}, u32[]{:S(2)}) collective-permute-start(bf16[4,128,256]{2,1,0:T(8,128)(2,1)S(1)} %get-tuple-element.104.refs_0_), channel_id=1, source_target_pairs={{8,0},{16,8},{24,16},{28,24},{20,28},{12,20},{4,12},{0,4},{9,1},{1... | collective-permute-start | bytes 786440 | tf_op jit(solution)/shard_map/ppermute | solution.py:307
  7.8 14.0 %collective-permute-start.7 = (bf16[4,128,256]{2,1,0:T(8,128)(2,1)S(1)}, bf16[4,128,256]{2,1,0:T(8,128)(2,1)}, u32[]{:S(2)}, u32[]{:S(2)}) collective-permute-start(bf16[4,128,256]{2,1,0:T(8,128)(2,1)S(1)} %get-tuple-element.104.refs_0_), channel_id=1, source_target_pairs={{0,8},{8,16},{16,24},{24,28},{28,20},{20,12},{12,4},{4,0},{1,9},{9... | collective-permute-start | bytes 786440 | tf_op jit(solution)/shard_map/ppermute | solution.py:310
  14.0 9.5 %collective-permute-start.2 = (bf16[4,128,256]{2,1,0:T(8,128)(2,1)}, bf16[4,128,256]{2,1,0:T(8,128)(2,1)S(1)}, u32[]{:S(2)}, u32[]{:S(2)}) collective-permute-start(bf16[4,128,256]{2,1,0:T(8,128)(2,1)} %collective-permute-done.refs_9_), channel_id=1, source_target_pairs={{8,0},{16,8},{24,16},{28,24},{20,28},{12,20},{4,12},{0,4},{9,1},{1... | collective-permute-start | bytes 786440 | tf_op jit(solution)/shard_map/ppermute | solution.py:307
  15.6 9.3 %collective-permute-start.3 = (bf16[4,128,256]{2,1,0:T(8,128)(2,1)}, bf16[4,128,256]{2,1,0:T(8,128)(2,1)S(1)}, u32[]{:S(2)}, u32[]{:S(2)}) collective-permute-start(bf16[4,128,256]{2,1,0:T(8,128)(2,1)} %collective-permute-done.1.refs_15_), channel_id=1, source_target_pairs={{0,8},{8,16},{16,24},{24,28},{28,20},{20,12},{12,4},{4,0},{1,9},{9... | collective-permute-start | bytes 786440 | tf_op jit(solution)/shard_map/ppermute | solution.py:310
  17.5 10.4 %collective-permute-start.5 = (bf16[4,128,256]{2,1,0:T(8,128)(2,1)S(1)}, bf16[4,128,256]{2,1,0:T(8,128)(2,1)S(1)}, u32[]{:S(2)}, u32[]{:S(2)}) collective-permute-start(bf16[4,128,256]{2,1,0:T(8,128)(2,1)S(1)} %collective-permute-done.4.refs_1_), channel_id=1, source_target_pairs={{8,0},{16,8},{24,16},{28,24},{20,28},{12,20},{4,12},{0,4},{9,1},{1... | collective-permute-start | bytes 786440 | tf_op jit(solution)/shard_map/ppermute | solution.py:307
  21.9 9.5 %collective-permute-start.8 = (bf16[4,128,256]{2,1,0:T(8,128)(2,1)}, bf16[4,128,256]{2,1,0:T(8,128)(2,1)S(1)}, u32[]{:S(2)}, u32[]{:S(2)}) collective-permute-start(bf16[4,128,256]{2,1,0:T(8,128)(2,1)} %collective-permute-done.7.refs_7_), channel_id=1, source_target_pairs={{0,8},{8,16},{16,24},{24,28},{28,20},{20,12},{12,4},{4,0},{1,9},{9... | collective-permute-start | bytes 786440 | tf_op jit(solution)/shard_map/ppermute | solution.py:310
  24.9 12.1 %collective-permute-start.12 = (bf16[4,128,256]{2,1,0:T(8,128)(2,1)S(1)}, bf16[4,128,256]{2,1,0:T(8,128)(2,1)S(1)}, u32[]{:S(2)}, u32[]{:S(2)}) collective-permute-start(bf16[4,128,256]{2,1,0:T(8,128)(2,1)S(1)} %collective-permute-done.3.refs_14_), channel_id=1, source_target_pairs={{0,8},{8,16},{16,24},{24,28},{28,20},{20,12},{12,4},{4,0},{1,9},{9... | collective-permute-start | bytes 786440 | tf_op jit(solution)/shard_map/ppermute | solution.py:310
  27.9 9.2 %collective-permute-start.6 = (bf16[4,128,256]{2,1,0:T(8,128)(2,1)S(1)}, bf16[4,128,256]{2,1,0:T(8,128)(2,1)S(1)}, u32[]{:S(2)}, u32[]{:S(2)}) collective-permute-start(bf16[4,128,256]{2,1,0:T(8,128)(2,1)S(1)} %collective-permute-done.5.refs_2_), channel_id=1, source_target_pairs={{8,0},{16,8},{24,16},{28,24},{20,28},{12,20},{4,12},{0,4},{9,1},{1... | collective-permute-start | bytes 786440 | tf_op jit(solution)/shard_map/ppermute | solution.py:307
  29.6 13.2 %collective-permute-start.11 = (bf16[4,128,256]{2,1,0:T(8,128)(2,1)S(1)}, bf16[4,128,256]{2,1,0:T(8,128)(2,1)S(1)}, u32[]{:S(2)}, u32[]{:S(2)}) collective-permute-start(bf16[4,128,256]{2,1,0:T(8,128)(2,1)S(1)} %collective-permute-done.2.refs_10_), channel_id=1, source_target_pairs={{8,0},{16,8},{24,16},{28,24},{20,28},{12,20},{4,12},{0,4},{9,1},{1... | collective-permute-start | bytes 786440 | tf_op jit(solution)/shard_map/ppermute | solution.py:307
  31.4 13.4 %collective-permute-start.9 = (bf16[4,128,256]{2,1,0:T(8,128)(2,1)S(1)}, bf16[4,128,256]{2,1,0:T(8,128)(2,1)S(1)}, u32[]{:S(2)}, u32[]{:S(2)}) collective-permute-start(bf16[4,128,256]{2,1,0:T(8,128)(2,1)S(1)} %collective-permute-done.8.refs_6_), channel_id=1, source_target_pairs={{0,8},{8,16},{16,24},{24,28},{28,20},{20,12},{12,4},{4,0},{1,9},{9... | collective-permute-start | bytes 786440 | tf_op jit(solution)/shard_map/ppermute | solution.py:310
  37.0 11.2 %collective-permute-start.13 = (bf16[4,128,256]{2,1,0:T(8,128)(2,1)S(1)}, bf16[4,128,256]{2,1,0:T(8,128)(2,1)S(1)}, u32[]{:S(2)}, u32[]{:S(2)}) collective-permute-start(bf16[4,128,256]{2,1,0:T(8,128)(2,1)S(1)} %collective-permute-done.12.refs_13_), channel_id=1, source_target_pairs={{0,8},{8,16},{16,24},{24,28},{28,20},{20,12},{12,4},{4,0},{1,9},{9... | collective-permute-start | bytes 786440 | tf_op jit(solution)/shard_map/ppermute | solution.py:310
  37.2 11.2 %collective-permute-start.10 = (bf16[4,128,256]{2,1,0:T(8,128)(2,1)S(1)}, bf16[4,128,256]{2,1,0:T(8,128)(2,1)S(1)}, u32[]{:S(2)}, u32[]{:S(2)}) collective-permute-start(bf16[4,128,256]{2,1,0:T(8,128)(2,1)S(1)} %collective-permute-done.6.refs_3_), channel_id=1, source_target_pairs={{8,0},{16,8},{24,16},{28,24},{20,28},{12,20},{4,12},{0,4},{9,1},{1... | collective-permute-start | bytes 786440 | tf_op jit(solution)/shard_map/ppermute | solution.py:307
  42.8 14.7 %collective-permute-start.15 = (bf16[4,128,256]{2,1,0:T(8,128)(2,1)S(1)}, bf16[4,128,256]{2,1,0:T(8,128)(2,1)S(1)}, u32[]{:S(2)}, u32[]{:S(2)}) collective-permute-start(bf16[4,128,256]{2,1,0:T(8,128)(2,1)S(1)} %get-tuple-element.64.refs_8_), channel_id=1, source_target_pairs={{8,0},{16,8},{24,16},{28,24},{20,28},{12,20},{4,12},{0,4},{9,1},{1... | collective-permute-start | bytes 786440 | tf_op jit(solution)/shard_map/ppermute | solution.py:307
  44.4 13.1 %collective-permute-start.17 = (bf16[4,128,256]{2,1,0:T(8,128)(2,1)S(1)}, bf16[4,128,256]{2,1,0:T(8,128)(2,1)S(1)}, u32[]{:S(2)}, u32[]{:S(2)}) collective-permute-start(bf16[4,128,256]{2,1,0:T(8,128)(2,1)S(1)} %get-tuple-element.64.refs_8_), channel_id=1, source_target_pairs={{0,8},{8,16},{16,24},{24,28},{28,20},{20,12},{12,4},{4,0},{1,9},{9... | collective-permute-start | bytes 786440 | tf_op jit(solution)/shard_map/ppermute | solution.py:310
  44.8 12.7 %collective-permute-start.14 = (bf16[4,128,256]{2,1,0:T(8,128)(2,1)S(1)}, bf16[4,128,256]{2,1,0:T(8,128)(2,1)S(1)}, u32[]{:S(2)}, u32[]{:S(2)}) collective-permute-start(bf16[4,128,256]{2,1,0:T(8,128)(2,1)S(1)} %get-tuple-element.80.refs_0_), channel_id=1, source_target_pairs={{8,0},{16,8},{24,16},{28,24},{20,28},{12,20},{4,12},{0,4},{9,1},{1... | collective-permute-start | bytes 786440 | tf_op jit(solution)/shard_map/ppermute | solution.py:307
  48.3 9.3 %collective-permute-start.16 = (bf16[4,128,256]{2,1,0:T(8,128)(2,1)S(1)}, bf16[4,128,256]{2,1,0:T(8,128)(2,1)S(1)}, u32[]{:S(2)}, u32[]{:S(2)}) collective-permute-start(bf16[4,128,256]{2,1,0:T(8,128)(2,1)S(1)} %get-tuple-element.80.refs_0_), channel_id=1, source_target_pairs={{0,8},{8,16},{16,24},{24,28},{28,20},{20,12},{12,4},{4,0},{1,9},{9... | collective-permute-start | bytes 786440 | tf_op jit(solution)/shard_map/ppermute | solution.py:310
  59.3 8.6 %collective-permute-start.19 = (bf16[256,512]{1,0:T(8,128)(2,1)S(1)}, bf16[256,512]{1,0:T(8,128)(2,1)S(1)}, u32[]{:S(2)}, u32[]{:S(2)}) collective-permute-start(bf16[256,512]{1,0:T(8,128)(2,1)S(1)} %fusion), channel_id=1, source_target_pairs={{0,2},{1,3},{2,0},{3,1},{4,6},{5,7},{6,4},{7,5},{8,10},{9,11},{10,... | collective-permute-start | bytes 786440 | tf_op jit(solution)/shard_map/ppermute | solution.py:376
  61.2 9.2 %collective-permute-start.20 = (bf16[4,128,256]{2,1,0:T(8,128)(2,1)S(1)}, bf16[4,128,256]{2,1,0:T(8,128)(2,1)S(1)}, u32[]{:S(2)}, u32[]{:S(2)}) collective-permute-start(bf16[4,128,256]{2,1,0:T(8,128)(2,1)S(1)} %collective-permute-done.14.refs_1_), channel_id=1, source_target_pairs={{8,0},{16,8},{24,16},{28,24},{20,28},{12,20},{4,12},{0,4},{9,1},{1... | collective-permute-start | bytes 786440 | tf_op jit(solution)/shard_map/ppermute | solution.py:307
  62.8 12.2 %collective-permute-start.21 = (bf16[4,128,256]{2,1,0:T(8,128)(2,1)S(1)}, bf16[4,128,256]{2,1,0:T(8,128)(2,1)S(1)}, u32[]{:S(2)}, u32[]{:S(2)}) collective-permute-start(bf16[4,128,256]{2,1,0:T(8,128)(2,1)S(1)} %collective-permute-done.15.refs_9_), channel_id=1, source_target_pairs={{8,0},{16,8},{24,16},{28,24},{20,28},{12,20},{4,12},{0,4},{9,1},{1... | collective-permute-start | bytes 786440 | tf_op jit(solution)/shard_map/ppermute | solution.py:307
  64.4 10.6 %collective-permute-start.22 = (bf16[4,128,256]{2,1,0:T(8,128)(2,1)S(1)}, bf16[4,128,256]{2,1,0:T(8,128)(2,1)S(1)}, u32[]{:S(2)}, u32[]{:S(2)}) collective-permute-start(bf16[4,128,256]{2,1,0:T(8,128)(2,1)S(1)} %collective-permute-done.16.refs_7_), channel_id=1, source_target_pairs={{0,8},{8,16},{16,24},{24,28},{28,20},{20,12},{12,4},{4,0},{1,9},{9... | collective-permute-start | bytes 786440 | tf_op jit(solution)/shard_map/ppermute | solution.py:310
  64.8 12.7 %collective-permute-start.23 = (bf16[4,128,256]{2,1,0:T(8,128)(2,1)S(1)}, bf16[4,128,256]{2,1,0:T(8,128)(2,1)S(1)}, u32[]{:S(2)}, u32[]{:S(2)}) collective-permute-start(bf16[4,128,256]{2,1,0:T(8,128)(2,1)S(1)} %collective-permute-done.17.refs_15_), channel_id=1, source_target_pairs={{0,8},{8,16},{16,24},{24,28},{28,20},{20,12},{12,4},{4,0},{1,9},{9... | collective-permute-start | bytes 786440 | tf_op jit(solution)/shard_map/ppermute | solution.py:310
  77.6 12.0 %collective-permute-start.25 = (bf16[4,128,256]{2,1,0:T(8,128)(2,1)S(1)}, bf16[4,128,256]{2,1,0:T(8,128)(2,1)S(1)}, u32[]{:S(2)}, u32[]{:S(2)}) collective-permute-start(bf16[4,128,256]{2,1,0:T(8,128)(2,1)S(1)} %collective-permute-done.20.refs_2_), channel_id=1, source_target_pairs={{8,0},{16,8},{24,16},{28,24},{20,28},{12,20},{4,12},{0,4},{9,1},{1... | collective-permute-start | bytes 786440 | tf_op jit(solution)/shard_map/ppermute | solution.py:307
  79.3 12.7 %collective-permute-start.26 = (bf16[4,128,256]{2,1,0:T(8,128)(2,1)S(1)}, bf16[4,128,256]{2,1,0:T(8,128)(2,1)S(1)}, u32[]{:S(2)}, u32[]{:S(2)}) collective-permute-start(bf16[4,128,256]{2,1,0:T(8,128)(2,1)S(1)} %collective-permute-done.21.refs_10_), channel_id=1, source_target_pairs={{8,0},{16,8},{24,16},{28,24},{20,28},{12,20},{4,12},{0,4},{9,1},{1... | collective-permute-start | bytes 786440 | tf_op jit(solution)/shard_map/ppermute | solution.py:307
  80.8 11.1 %collective-permute-start.27 = (bf16[4,128,256]{2,1,0:T(8,128)(2,1)S(1)}, bf16[4,128,256]{2,1,0:T(8,128)(2,1)S(1)}, u32[]{:S(2)}, u32[]{:S(2)}) collective-permute-start(bf16[4,128,256]{2,1,0:T(8,128)(2,1)S(1)} %collective-permute-done.22.refs_6_), channel_id=1, source_target_pairs={{0,8},{8,16},{16,24},{24,28},{28,20},{20,12},{12,4},{4,0},{1,9},{9... | collective-permute-start | bytes 786440 | tf_op jit(solution)/shard_map/ppermute | solution.py:310
  81.3 13.3 %collective-permute-start.28 = (bf16[4,128,256]{2,1,0:T(8,128)(2,1)S(1)}, bf16[4,128,256]{2,1,0:T(8,128)(2,1)S(1)}, u32[]{:S(2)}, u32[]{:S(2)}) collective-permute-start(bf16[4,128,256]{2,1,0:T(8,128)(2,1)S(1)} %collective-permute-done.23.refs_14_), channel_id=1, source_target_pairs={{0,8},{8,16},{16,24},{24,28},{28,20},{20,12},{12,4},{4,0},{1,9},{9... | collective-permute-start | bytes 786440 | tf_op jit(solution)/shard_map/ppermute | solution.py:310
  94.6 10.2 %collective-permute-start.29 = (bf16[4,128,256]{2,1,0:T(8,128)(2,1)S(1)}, bf16[4,128,256]{2,1,0:T(8,128)(2,1)S(1)}, u32[]{:S(2)}, u32[]{:S(2)}) collective-permute-start(bf16[4,128,256]{2,1,0:T(8,128)(2,1)S(1)} %collective-permute-done.25.refs_3_), channel_id=1, source_target_pairs={{8,0},{16,8},{24,16},{28,24},{20,28},{12,20},{4,12},{0,4},{9,1},{1... | collective-permute-start | bytes 786440 | tf_op jit(solution)/shard_map/ppermute | solution.py:307
  95.1 9.7 %collective-permute-start.30 = (bf16[4,128,256]{2,1,0:T(8,128)(2,1)S(1)}, bf16[4,128,256]{2,1,0:T(8,128)(2,1)S(1)}, u32[]{:S(2)}, u32[]{:S(2)}) collective-permute-start(bf16[4,128,256]{2,1,0:T(8,128)(2,1)S(1)} %collective-permute-done.28.refs_13_), channel_id=1, source_target_pairs={{0,8},{8,16},{16,24},{24,28},{28,20},{20,12},{12,4},{4,0},{1,9},{9... | collective-permute-start | bytes 786440 | tf_op jit(solution)/shard_map/ppermute | solution.py:310
  116.7 8.4 %collective-permute-start.32 = (bf16[256,512]{1,0:T(8,128)(2,1)S(1)}, bf16[256,512]{1,0:T(8,128)(2,1)S(1)}, u32[]{:S(2)}, u32[]{:S(2)}) collective-permute-start(bf16[256,512]{1,0:T(8,128)(2,1)S(1)} %fusion.1), channel_id=1, source_target_pairs={{0,2},{1,3},{2,0},{3,1},{4,6},{5,7},{6,4},{7,5},{8,10},{9,11},{10,... | collective-permute-start | bytes 786440 | tf_op jit(solution)/shard_map/ppermute | solution.py:376
  128.1 30.7 %collective-permute-start.35 = (bf16[256,256]{1,0:T(8,128)(2,1)}, bf16[256,256]{1,0:T(8,128)(2,1)S(1)}, u32[]{:S(2)}, u32[]{:S(2)}) collective-permute-start(bf16[256,256]{1,0:T(8,128)(2,1)} %fusion.6), channel_id=1, source_target_pairs={{0,2},{1,3},{2,0},{3,1},{4,6},{5,7},{6,4},{7,5},{8,10},{9,11},{10,... | collective-permute-start | bytes 393224 | tf_op jit(solution)/shard_map/ppermute | solution.py:376
  153.4 6.4 %collective-permute-start.36 = (bf16[2,256,256]{2,1,0:T(8,128)(2,1)}, bf16[2,256,256]{2,1,0:T(8,128)(2,1)}, u32[]{:S(2)}, u32[]{:S(2)}) collective-permute-start(bf16[2,256,256]{2,1,0:T(8,128)(2,1)} %get-tuple-element.95), channel_id=1, source_target_pairs={{0,1},{1,0},{2,3},{3,2},{4,5},{5,4},{6,7},{7,6},{8,9},{9,8},{10,11... | collective-permute-start | bytes 786440 | tf_op jit(solution)/shard_map/ppermute | solution.py:429
  (44 other events, 591.9 us)
where the time goes:
time: 168 us
  Pallas kernels  68.3 us (41%)
  waiting for transfers between devices  45.8 us (27%)
  starting transfers between devices  34.3 us (20%)
  local copies, waits for them, and re-layouts  12.8 us (8%)
  other arithmetic  5.54 us (3%)
    pallas_call x11, Pallas kernels, run(): pl.pallas_call(kernel, out_shape=shapes, in_specs=[smem] * len(scalars) +...  68.3 us
    ppermute x14, starting transfers between devices, step(): self.up[t] = lax.ppermute(self.up[t], self.axis, self.ahead)  23.7 us
    ppermute x14, waiting for transfers between devices, step(): self.up[t] = lax.ppermute(self.up[t], self.axis, self.ahead)  19.3 us
    ppermute x14, waiting for transfers between devices, step(): self.down[t] = lax.ppermute(self.down[t], self.axis, self.behind)  16.1 us
    unnamed x76, local copies, waits for them, and re-layouts  8.06 us
    ppermute x4, waiting for transfers between devices, shifted(): lax.ppermute(x, 'cols', [(i, (i + 2 * shift) % cols) for i in range(cols)])  6.48 us
    ppermute x14, starting transfers between devices, step(): self.down[t] = lax.ppermute(self.down[t], self.axis, self.behind)  5.22 us
    ppermute x4, starting transfers between devices, shifted(): lax.ppermute(x, 'cols', [(i, (i + 2 * shift) % cols) for i in range(cols)])  4.99 us
  transfers between devices with their start and end apart: 38, of which 23 were waited for; matrix products, arithmetic and copies ran while one was open for 4% of the time, Pallas kernels for 35%

commit v1 on v0

--- a/solution.py
+++ b/solution.py
@@ -171,43 +171,39 @@
     apply_factor(info, y, work, qt, basis, q)
 
 
-def fetch(blocks, buffer, sems, which):
-    slab = blocks[0].shape[1]
-    return [
-        [
-            pltpu.make_async_copy(b.at[j], buffer.at[j, pl.ds(n * slab, slab)], sems.at[which, j, n])
-            for n, b in enumerate(blocks)
-        ]
-        for j in range(buffer.shape[0])
-    ]
-
-
-def update_kernel(blocks, info, ranks, panel_vt, sampler_t, panel_u, *refs):
-    u, v = refs[:blocks], refs[blocks : 2 * blocks]
-    cross, give, keep, u_buf, v_buf, sems = refs[2 * blocks :]
-    priors, order, width = u_buf.shape
+def gather_kernel(places, blocks, info, panel_vt, sampler_t, *refs):
+    new = len(places)
+    u, v = refs[:new], refs[new : 2 * new]
+    kept = refs[2 * new : -3]
+    sampled, met, u_all = refs[-3:]
+    priors, order, width = u_all.shape
     slab = order // blocks
+    spans = [pl.ds(pl.multiple_of(info[2 + p] * slab, 128), slab) for p in places]
+    drawn = jnp.concatenate([sampler_t[:, span] for span in spans], 1)
+    for j in range(priors):
+        left = jnp.concatenate([panel_vt[j, :, span] for span in spans], 1)
+        u_new = jnp.concatenate([block[j] for block in u], 0)
+        v_new = jnp.concatenate([block[j] for block in v], 0)
+        one, two = dot(drawn, u_new), dot(left, v_new)
+        if kept:
+            one, two = one + kept[0][j], two + kept[1][j]
+        sampled[j] = one
+        met[j] = two
+        for n, p in enumerate(places):
+            u_all[j, p * slab : (p + 1) * slab, :] = u_new[n * slab : (n + 1) * slab, :]
+
+
+def update_kernel(info, ranks, sampled, met, panel_u, cross, give, keep):
+    priors, width, _ = cross.shape
     half = keep.shape[1]
     core = info[0]
-    copies = [fetch(u, u_buf, sems, 0), fetch(v, v_buf, sems, 1)]
-    for j in range(priors):
-        for t in range(2):
-            for copy in copies[t][j]:
-                copy.start()
-    spans = [pl.ds(pl.multiple_of(info[2 + b] * slab, 128), slab) for b in range(blocks)]
     row = lax.broadcasted_iota(jnp.int32, (width, width), 0)
     col = lax.broadcasted_iota(jnp.int32, (width, width), 1)
-    drawn = jnp.concatenate([sampler_t[:, span] for span in spans], 1)
     terms = []
     for j in range(priors):
-        for t in range(2):
-            for copy in copies[t][j]:
-                copy.wait()
-        sampled = dot(drawn, u_buf[j])
-        met = dot(jnp.concatenate([panel_vt[j, :, span] for span in spans], 1), v_buf[j])
-        met = jnp.where((row < ranks[0, j]) & (col < ranks[1, j]), met, 0.0).astype(BF16)
-        cross[j] = met
-        terms.append(dot11(sampled.astype(BF16), met).astype(BF16))
+        inside = (row < ranks[0, j]) & (col < ranks[1, j])
+        cross[j] = jnp.where(inside, met[j], 0.0).astype(BF16)
+        terms.append(dot11(sampled[j].astype(BF16), cross[j]).astype(BF16))
     for out, which in ((give, 1 - core), (keep, core)):
         rows = pl.ds(pl.multiple_of(which * half, 128), half)
         total = jnp.zeros((width, half), F32)
@@ -216,29 +212,20 @@
         out[...] = total.astype(out.dtype)
 
 
-def project_kernel(blocks, info, qt, panel_u, cross, *refs):
-    u = refs[:blocks]
-    give, keep, work, u_buf, sems = refs[blocks:]
-    priors, order, width = u_buf.shape
+def project_kernel(blocks, info, qt, panel_u, cross, u_all, give, keep, work):
+    priors, order, width = u_all.shape
     slab = order // blocks
     pairs, share, _ = keep.shape
     core = info[0]
-    copies = fetch(u, u_buf, sems, 0)
-    for each in copies:
-        for copy in each:
-            copy.start()
     mids = []
     for j in range(priors):
         inner = dot(qt[...], panel_u[j]).astype(BF16)
         mids.append(dot(inner, cross[j]).astype(BF16))
-    for each in copies:
-        for copy in each:
-            copy.wait()
     some = max(1, blocks // 2)
     for begin in range(0, blocks, some):
         total = jnp.zeros((some * slab, width), F32)
         for j in range(priors):
-            total += dot11(u_buf[j, begin * slab : (begin + some) * slab, :], mids[j])
+            total += dot11(u_all[j, begin * slab : (begin + some) * slab, :], mids[j])
         for n in range(some):
             rows = pl.ds(pl.multiple_of(info[2 + begin + n] * slab, SUB), slab)
             work[rows, :] = total[n * slab : (n + 1) * slab, :]
@@ -269,21 +256,22 @@
         out[c] = dot11(proj, orig_u[c, rows, :])
 
 
-def run(kernel, scalars, arrays, outs, scratch, limit, flops, name, apart=()):
+def run(kernel, scalars, arrays, outs, scratch, limit, flops, name, aliases={}):
     smem = pl.BlockSpec(memory_space=pltpu.SMEM)
     vmem = pl.BlockSpec(memory_space=pltpu.VMEM)
     shapes = [jax.ShapeDtypeStruct(*o) for o in outs]
-    moved = sum(a.size * a.dtype.itemsize for a in list(arrays) + list(apart) + shapes)
+    moved = sum(a.size * a.dtype.itemsize for a in list(arrays) + shapes)
     return pl.pallas_call(
         kernel,
         out_shape=shapes,
-        in_specs=[smem] * len(scalars) + [vmem] * len(arrays) + [pl.BlockSpec(memory_space=pl.ANY)] * len(apart),
+        in_specs=[smem] * len(scalars) + [vmem] * len(arrays),
         out_specs=[vmem] * len(shapes),
         scratch_shapes=scratch,
+        input_output_aliases=aliases,
         compiler_params=pltpu.CompilerParams(vmem_limit_bytes=limit * MIB),
         cost_estimate=pl.CostEstimate(flops=flops, bytes_accessed=moved, transcendentals=0),
         name=name,
-    )(*scalars, *arrays, *apart)
+    )(*scalars, *arrays)
 
 
 def ring_order(count):
@@ -346,7 +334,9 @@
     ring = ring_order(count)
     place = np.argsort(np.array(ring))
     table = np.array([[ring[(place[r] + d) % count] for d in range(count)] for r in range(count)], np.int32)
-    if count > RING_MOST:
+    last = count // 2
+    whole = count % 2 == 1 or last < 4 or count > RING_MOST
+    if whole:
         table = np.zeros((count, 1), np.int32)
     sources = jnp.asarray(table)[lax.axis_index("rows")]
     info = jnp.concatenate([jnp.stack([core, me]).astype(jnp.int32), sources])
@@ -357,100 +347,150 @@
         turn_kernel, [], [panel_v, sampler], [((priors, width, order), BF16), ((sampler.shape[1], order), BF16)], [], 12,
         10 * square * order, "turn"
     )
-    whole = count > RING_MOST
-    if not whole:
-        now = Ring([pivot_u[0], pivot_v[0]], ring, "rows")
-        now.step(1)
-        panel_vt = now.tie(panel_vt, 1, (1,))
-        now.step(2)
     (start,) = run(
         start_kernel, [info], [sampler_t, orig_u, orig_v], [((pivots, width, half), F32)], [], 12,
         pivots * square * (order + half), "start"
     )
-    if not whole:
-        start = now.tie(start, 2, (1,))
-        for number in range(3, count // 2 + 1):
-            now.step(number)
 
     def shifted(x, shift):
         return lax.ppermute(x, "cols", [(i, (i + 2 * shift) % cols) for i in range(cols)])
 
-    buffer = pltpu.VMEM((priors, order, width), BF16)
     matrix = pltpu.VMEM((width, width), F32)
     tall = pltpu.VMEM((width, order), F32)
 
-    def updated(c, blocks_u, blocks_v):
-        blocks = len(blocks_u)
+    def gathered(places, blocks, new_u, new_v, kept):
+        new = len(places)
+        shapes = [((priors, width, width), F32), ((priors, width, width), F32), ((priors, order, width), BF16)]
+        first = 3 + 2 * new
+        return run(
+            functools.partial(gather_kernel, places, blocks), [info], [panel_vt, sampler_t, *new_u, *new_v, *kept],
+            shapes, [], 20, 2 * priors * square * order * new // blocks, "gather",
+            {first + n: n for n in range(len(kept))}
+        )
+
+    def taken(source, number, kept):
+        places = sorted({number, count - number} | ({0} if number == 1 else set()))
+        new_u, new_v = ([source.found[t][p] for p in places] for t in range(2))
+        return gathered(places, count, new_u, new_v, kept)
+
+    def updated(c, sampled, met):
         ranks = jnp.stack([panel_rank[0], pivot_rank[c]])
         return run(
-            functools.partial(update_kernel, blocks), [info, ranks], [panel_vt, sampler_t, panel_u],
+            update_kernel, [info, ranks], [sampled, met, panel_u],
             [((priors, width, width), BF16), ((width, half), BF16), ((width, half), F32)],
-            [buffer, buffer, pltpu.SemaphoreType.DMA((2, priors, blocks))], 20,
-            3 * priors * square * (3 * order + width), "update", (*blocks_u, *blocks_v)
+            [], 16, 2 * priors * square * (order + width), "update"
         )
 
-    def finished(c, blocks_u, cross, give, keep, beside):
-        blocks = len(blocks_u)
+    def summed(c, give, keep, beside, outs=()):
         chip = keep + lax.ppermute(give, "cols", swap).astype(F32)
         sent = chip.astype(BF16)
         for shift in range(1, pairs):
             chip = chip + shifted(sent, shift).astype(F32)
         if beside is not None:
-            chip = beside.tie(chip, 2)
-            beside.step(3)
+            chip = beside.hold(beside.hold(chip, 1, 2), 0, 3)
+        chip, *outs = lax.optimization_barrier((chip, *outs))
         ymine = start[c] - chip
         yother = lax.ppermute(ymine, "cols", swap)
-        finals = [((width, order), BF16), ((share, width), F32)]
-        if beside is None:
-            qt, rows = run(
-                orthonormal_kernel, [info], [ymine, yother], finals, [tall, matrix], 12, 128 * square * order, "orthonormal"
-            )
-        else:
-            yt, work = run(
-                first_kernel, [info], [ymine, yother], [((width, order), F32), ((width, width), F32)], [matrix], 12,
-                64 * square * order, "orthonormal_first"
-            )
-            work = beside.tie(work, 3)
-            beside.step(4)
-            qt, rows = run(
-                last_kernel, [info], [yt, work], finals, [tall, matrix], 12, 64 * square * order, "orthonormal_last"
-            )
-            beside.found[0][0], qt = lax.optimization_barrier((beside.found[0][0], qt))
+        return ymine, yother, outs
+
+    finals = [((width, order), BF16), ((share, width), F32)]
+
+    def projected(c, blocks, qt, cross, u_all):
         give, keep = run(
-            functools.partial(project_kernel, blocks), [info], [qt, panel_u, cross],
+            functools.partial(project_kernel, blocks), [info], [qt, panel_u, cross, u_all],
             [((pairs, share, width), BF16), ((pairs, share, width), F32)],
-            [pltpu.VMEM((order, width), F32), buffer, pltpu.SemaphoreType.DMA((1, priors, blocks))], 16,
-            3 * priors * square * (2 * order + width), "project", blocks_u
+            [pltpu.VMEM((order, width), F32)], 16, 2 * priors * square * (2 * order + width), "project"
         )
         (own,) = run(
             left_kernel, [info], [qt, orig_u[c], orig_v[c]], [((share, width), F32)], [], 8,
             square * (order + share), "left"
         )
+        return give, keep, own
+
+    def halved(give, keep, own):
         chip = keep + lax.ppermute(give, "cols", swap).astype(F32)
-        total = lax.dynamic_index_in_dim(chip, pair, 0, False)
-        for shift in range(1, pairs):
-            sent = lax.dynamic_index_in_dim(chip, (pair + shift) % pairs, 0, False).astype(BF16)
-            total = total + shifted(sent, shift).astype(F32)
-        return rows, own - total
-
-    results = []
+        total = own - lax.dynamic_index_in_dim(chip, pair, 0, False)
+        sent = [
+            lax.dynamic_index_in_dim(chip, (pair + shift) % pairs, 0, False).astype(BF16) for shift in range(1, pairs)
+        ]
+        return total, *sent
+
+    def closed(total, *sent):
+        for shift, each in enumerate(sent, 1):
+            total = total - shifted(each, shift).astype(F32)
+        return total
+
+    def orthonormal(ymine, yother):
+        return run(
+            orthonormal_kernel, [info], [ymine, yother], finals, [tall, matrix], 12, 128 * square * order, "orthonormal"
+        )
+
+    basis, coeff = [], []
     if whole:
         for c in range(pivots):
-            blocks_u, blocks_v = ([lax.all_gather(x[c], "rows", axis=1, tiled=True)] for x in (pivot_u, pivot_v))
-            results.append(finished(c, blocks_u, *updated(c, blocks_u, blocks_v), None))
+            new_u, new_v = ([lax.all_gather(x[c], "rows", axis=1, tiled=True)] for x in (pivot_u, pivot_v))
+            sampled, met, u_all = gathered([0], 1, new_u, new_v, [])
+            cross, give, keep = updated(c, sampled, met)
+            ymine, yother, _ = summed(c, give, keep, None)
+            qt, rows = orthonormal(ymine, yother)
+            basis.append(rows)
+            coeff.append(closed(*halved(*projected(c, 1, qt, cross, u_all))))
     else:
+        now, kept = Ring([pivot_u[0], pivot_v[0]], ring, "rows"), []
+        number = 1
+        parts = None
         for c in range(pivots):
             later = None
-            if c + 1 < pivots:
-                later = Ring([now.hold(pivot_u[c + 1], 0, now.near), now.hold(pivot_v[c + 1], 1, now.near)], ring, "rows")
-                later.step(1)
-            cross, give, keep = updated(c, now.blocks(0), now.blocks(1))
+            while number <= last:
+                if number == last and c + 1 < pivots:
+                    later = Ring(
+                        [now.hold(pivot_u[c + 1], 0, last - 2), now.hold(pivot_v[c + 1], 1, last - 2)], ring, "rows"
+                    )
+                    later.step(1)
+                    now.up[0] = later.hold(now.up[0], 0, 1)
+                    now.down[1] = later.hold(now.down[1], 1, 1)
+                now.step(number)
+                if c == 0 and number < last:
+                    if number == 2:
+                        start = now.tie(start, 2, (1,))
+                    if number > 1:
+                        kept[0] = now.tie(kept[0], number, (0,))
+                kept = list(taken(now, number, kept))
+                number += 1
+            if parts is not None:
+                kept[1], *parts = lax.optimization_barrier((kept[1], *parts))
+            sampled, met, u_all = kept
+            cross, give, keep = updated(c, sampled, met)
+            kept = []
             if later is not None:
-                give = later.tie(give, 1)
+                kept = list(taken(later, 1, kept))
                 later.step(2)
-            results.append(finished(c, now.blocks(0), cross, give, keep, later))
-            now = later
-    basis, coeff = zip(*results)
+                give = later.tie(give, 2, (0,))
+                kept[0] = later.tie(kept[0], 2, (1,))
+                later.step(3)
+                kept = list(taken(later, 2, kept))
+            outs = projected(c - 1, count, *parts) if parts is not None and later is None else ()
+            ymine, yother, outs = summed(c, give, keep, later, outs)
+            if later is None:
+                if outs:
+                    yother, *outs = lax.optimization_barrier((yother, *halved(*outs)))
+                    coeff.append(closed(*outs))
+                qt, rows = orthonormal(ymine, yother)
+                coeff.append(closed(*halved(*projected(c, count, qt, cross, u_all))))
+            else:
+                yt, work = run(
+                    first_kernel, [info], [ymine, yother], [((width, order), F32), ((width, width), F32)], [matrix], 12,
+                    64 * square * order, "orthonormal_first"
+                )
+                work = later.tie(work, 3, (1,))
+                kept[0] = later.tie(kept[0], 3, (0,))
+                qt, rows = run(
+                    last_kernel, [info], [yt, work], finals, [tall, matrix], 12, 64 * square * order, "orthonormal_last"
+                )
+                kept = list(taken(later, 3, [*kept[:2], kept[2]])) if last > 3 else kept
+                parts = [qt, cross, u_all]
+            basis.append(rows)
+            now, number = later, 4
     return (jnp.stack(basis)[:, None], jnp.stack(coeff)[:, None])
 
 

time: 168 us -> 157 us (0.935)
  Pallas kernels: 68.3 us -> 53.4 us
  waiting for transfers between devices: 45.8 us -> 47.6 us
    pallas_call x11 -> x19, Pallas kernels: 68.3 us -> 53.4 us  [run(): pl.pallas_call(kernel, out_shape=shapes, in_specs=[smem] * len(scalars) +...]
    ppermute x14, waiting for transfers between devices: 16.1 us -> 21.4 us  [step(): self.down[t] = lax.ppermute(self.down[t], self.axis, self.behind)]
    ppermute x4, waiting for transfers between devices: 6.48 us -> 4.32 us  [shifted(): lax.ppermute(x, 'cols', [(i, (i + 2 * shift) % cols) for i in range(cols)])]
    ppermute x14, starting transfers between devices: 23.7 us -> 25.6 us  [step(): self.up[t] = lax.ppermute(self.up[t], self.axis, self.ahead)]
    unnamed x76 -> x54, local copies, waits for them, and re-layouts: 8.06 us -> 9.26 us
  transfers between devices with their start and end apart: 38 -> 38, of which waited for: 23 -> 20; matrix products, arithmetic and copies ran while one was open for 4% -> 3% of each run, Pallas kernels for 35% -> 21%
where the time goes in v1:
time: 157 us; the launch traced here: 156 us
  Pallas kernels  53.4 us (34%)
  waiting for transfers between devices  47.6 us (30%)
  starting transfers between devices  35.8 us (23%)
  local copies, waits for them, and re-layouts  14.3 us (9%)
  other arithmetic  4.19 us (3%)
    pallas_call x19, Pallas kernels, run(): pl.pallas_call(kernel, out_shape=shapes, in_specs=[smem] * len(scalars) +...  53.4 us
    ppermute x14, starting transfers between devices, step(): self.up[t] = lax.ppermute(self.up[t], self.axis, self.ahead)  25.6 us
    ppermute x14, waiting for transfers between devices, step(): self.down[t] = lax.ppermute(self.down[t], self.axis, self.behind)  21.4 us
    ppermute x14, waiting for transfers between devices, step(): self.up[t] = lax.ppermute(self.up[t], self.axis, self.ahead)  18.9 us
    unnamed x54, local copies, waits for them, and re-layouts  9.26 us
    ppermute x4, starting transfers between devices, shifted(): lax.ppermute(x, 'cols', [(i, (i + 2 * shift) % cols) for i in range(cols)])  5.2 us
    ppermute x4, waiting for transfers between devices, shifted(): lax.ppermute(x, 'cols', [(i, (i + 2 * shift) % cols) for i in range(cols)])  4.32 us
    ppermute x14, starting transfers between devices, step(): self.down[t] = lax.ppermute(self.down[t], self.axis, self.behind)  3.74 us
  transfers between devices with their start and end apart: 38, of which 20 were waited for; matrix products, arithmetic and copies ran while one was open for 3% of the time, Pallas kernels for 21%

profile of v1, /device:TPU:0, one launch (start us, length us, event | category | flops | bytes accessed | tf_op | source)
XLA Modules:
  0.0 156.4 jit_solution(6065811079842416465)
XLA Ops:
  1.9 3.0 %collective-permute-start.4 = (bf16[4,128,256]{2,1,0:T(8,128)(2,1)S(1)}, bf16[4,128,256]{2,1,0:T(8,128)(2,1)S(1)}, u32[]{:S(2)}, u32[]{:S(2)}) collective-permute-start(bf16[4,128,256]{2,1,0:T(8,128)(2,1)S(1)} %get-tuple-element.179.refs_0_), channel_id=1, source_target_pairs={{8,0},{16,8},{24,16},{28,24},{20,28},{12,20},{4,12},{0,4},{9,1},{1... | collective-permute-start | bytes 786440 | tf_op jit(solution)/shard_map/ppermute | solution.py:295
  5.0 1.8 %slice_bitcast_fusion.4 = (bf16[4,128,256]{2,1,0:T(8,128)(2,1)}, bf16[4,128,256]{2,1,0:T(8,128)(2,1)S(1)}) fusion(bf16[2,4,128,256]{3,2,1,0:T(8,128)(2,1)} %param.14), kind=kLoop, calls=%fused_computation.23 | loop fusion | bytes 1048576 | tf_op jit(solution)/shard_map/squeeze | solution.py:447
  6.8 1.9 %collective-permute-start = (bf16[4,128,256]{2,1,0:T(8,128)(2,1)S(1)}, bf16[4,128,256]{2,1,0:T(8,128)(2,1)}, u32[]{:S(2)}, u32[]{:S(2)}) collective-permute-start(bf16[4,128,256]{2,1,0:T(8,128)(2,1)S(1)} %get-tuple-element.177.refs_3_), channel_id=1, source_target_pairs={{8,0},{16,8},{24,16},{28,24},{20,28},{12,20},{4,12},{0,4},{9,1},{1... | collective-permute-start | bytes 786440 | tf_op jit(solution)/shard_map/ppermute | solution.py:295
  9.5 2.6 %collective-permute-done.4.refs_1_ = bf16[4,128,256]{2,1,0:T(8,128)(2,1)S(1)} collective-permute-done((bf16[4,128,256]{2,1,0:T(8,128)(2,1)S(1)}, bf16[4,128,256]{2,1,0:T(8,128)(2,1)S(1)}, u32[]{:S(2)}, u32[]{:S(2)}) %collective-permute-start.4) | collective-permute-done | bytes 262176 | tf_op jit(solution)/shard_map/ppermute | solution.py:295
  12.1 2.0 %collective-permute-start.6 = (bf16[4,128,256]{2,1,0:T(8,128)(2,1)S(1)}, bf16[4,128,256]{2,1,0:T(8,128)(2,1)S(1)}, u32[]{:S(2)}, u32[]{:S(2)}) collective-permute-start(bf16[4,128,256]{2,1,0:T(8,128)(2,1)S(1)} %collective-permute-done.4.refs_1_), channel_id=1, source_target_pairs={{8,0},{16,8},{24,16},{28,24},{20,28},{12,20},{4,12},{0,4},{9,1},{1... | collective-permute-start | bytes 786440 | tf_op jit(solution)/shard_map/ppermute | solution.py:295
  16.1 1.7 %collective-permute-done.refs_4_ = bf16[4,128,256]{2,1,0:T(8,128)(2,1)} collective-permute-done((bf16[4,128,256]{2,1,0:T(8,128)(2,1)S(1)}, bf16[4,128,256]{2,1,0:T(8,128)(2,1)}, u32[]{:S(2)}, u32[]{:S(2)}) %collective-permute-start) | collective-permute-done | bytes 262176 | tf_op jit(solution)/shard_map/ppermute | solution.py:295
  17.8 2.0 %collective-permute-start.1 = (bf16[4,128,256]{2,1,0:T(8,128)(2,1)}, bf16[4,128,256]{2,1,0:T(8,128)(2,1)S(1)}, u32[]{:S(2)}, u32[]{:S(2)}) collective-permute-start(bf16[4,128,256]{2,1,0:T(8,128)(2,1)} %collective-permute-done.refs_4_), channel_id=1, source_target_pairs={{8,0},{16,8},{24,16},{28,24},{20,28},{12,20},{4,12},{0,4},{9,1},{1... | collective-permute-start | bytes 786440 | tf_op jit(solution)/shard_map/ppermute | solution.py:295
  19.9 1.9 %gather.8 = (f32[4,256,256]{2,1,0:T(8,128)S(1)}, f32[4,256,256]{2,1,0:T(8,128)S(1)}, bf16[4,1024,256]{2,1,0:T(8,128)(2,1)S(1)}) custom-call(s32[10]{0:T(128)S(1)} %pad_add_fusion.2.info, bf16[4,256,1024]{2,1,0:T(8,128)(2,1)S(1)} %get-tuple-element.88.panel_vt, bf16[256,1024]{1,0:T(8,128)(2,1)S(1)} %get-tuple-element.86.sampler_t, ...), custom_call_target="tpu_custom_call" | custom-call | flops 402653184 | bytes 8388608 | tf_op jit(solution)/shard_map/gather/pallas_call | solution.py:264
  23.3 2.0 %collective-permute-done.7.refs_1_ = bf16[4,128,256]{2,1,0:T(8,128)(2,1)S(1)} collective-permute-done((bf16[4,128,256]{2,1,0:T(8,128)(2,1)S(1)}, bf16[4,128,256]{2,1,0:T(8,128)(2,1)S(1)}, u32[]{:S(2)}, u32[]{:S(2)}) %collective-permute-start.7) | collective-permute-done | bytes 262176 | tf_op jit(solution)/shard_map/ppermute | solution.py:298
  27.3 1.6 %start.1 = f32[2,256,512]{2,1,0:T(8,128)S(1)} custom-call(s32[10]{0:T(128)S(1)} %pad_add_fusion.2.info, bf16[256,1024]{1,0:T(8,128)(2,1)S(1)} %get-tuple-element.86.sampler_t, bf16[2,1024,256]{2,1,0:T(8,128)(2,1)S(1)} %bitcast.54, bf16[2,1024,256]{2,1,0:T(8,128)(2,1)S(1)} %bitcast.55), custom_call_target="tpu_custom_call" | custom-call | flops 402653184 | bytes 3670016 | tf_op jit(solution)/shard_map/start/pallas_call | solution.py:264
  29.0 2.0 %collective-permute-done.3.refs_3_ = bf16[4,128,256]{2,1,0:T(8,128)(2,1)S(1)} collective-permute-done((bf16[4,128,256]{2,1,0:T(8,128)(2,1)}, bf16[4,128,256]{2,1,0:T(8,128)(2,1)S(1)}, u32[]{:S(2)}, u32[]{:S(2)}) %collective-permute-start.3) | collective-permute-done | bytes 262176 | tf_op jit(solution)/shard_map/ppermute | solution.py:298
  31.0 1.9 %collective-permute-start.14 = (bf16[4,128,256]{2,1,0:T(8,128)(2,1)S(1)}, bf16[4,128,256]{2,1,0:T(8,128)(2,1)S(1)}, u32[]{:S(2)}, u32[]{:S(2)}) collective-permute-start(bf16[4,128,256]{2,1,0:T(8,128)(2,1)S(1)} %copy-done.10), channel_id=1, source_target_pairs={{8,0},{16,8},{24,16},{28,24},{20,28},{12,20},{4,12},{0,4},{9,1},{1... | collective-permute-start | bytes 786440 | tf_op jit(solution)/shard_map/ppermute | solution.py:295
  34.5 2.0 %collective-permute-start.10 = (bf16[4,128,256]{2,1,0:T(8,128)(2,1)S(1)}, bf16[4,128,256]{2,1,0:T(8,128)(2,1)S(1)}, u32[]{:S(2)}, u32[]{:S(2)}) collective-permute-start(bf16[4,128,256]{2,1,0:T(8,128)(2,1)S(1)} %get-tuple-element.99.refs_0_), channel_id=1, source_target_pairs={{8,0},{16,8},{24,16},{28,24},{20,28},{12,20},{4,12},{0,4},{9,1},{1... | collective-permute-start | bytes 786440 | tf_op jit(solution)/shard_map/ppermute | solution.py:295
  37.8 4.3 %collective-permute-done.13.refs_3_ = bf16[4,128,256]{2,1,0:T(8,128)(2,1)S(1)} collective-permute-done((bf16[4,128,256]{2,1,0:T(8,128)(2,1)S(1)}, bf16[4,128,256]{2,1,0:T(8,128)(2,1)S(1)}, u32[]{:S(2)}, u32[]{:S(2)}) %collective-permute-start.13) | collective-permute-done | bytes 262176 | tf_op jit(solution)/shard_map/ppermute | solution.py:298
  43.7 4.0 %collective-permute-done.15.refs_5_ = bf16[4,128,256]{2,1,0:T(8,128)(2,1)S(1)} collective-permute-done((bf16[4,128,256]{2,1,0:T(8,128)(2,1)S(1)}, bf16[4,128,256]{2,1,0:T(8,128)(2,1)S(1)}, u32[]{:S(2)}, u32[]{:S(2)}) %collective-permute-start.15) | collective-permute-done | bytes 262176 | tf_op jit(solution)/shard_map/ppermute | solution.py:298
  47.9 5.5 %collective-permute-done.11.refs_2_ = bf16[4,128,256]{2,1,0:T(8,128)(2,1)S(1)} collective-permute-done((bf16[4,128,256]{2,1,0:T(8,128)(2,1)S(1)}, bf16[4,128,256]{2,1,0:T(8,128)(2,1)S(1)}, u32[]{:S(2)}, u32[]{:S(2)}) %collective-permute-start.11) | collective-permute-done | bytes 262176 | tf_op jit(solution)/shard_map/ppermute | solution.py:298
  59.0 2.6 %collective-permute-done.12.refs_0_ = bf16[4,128,256]{2,1,0:T(8,128)(2,1)S(1)} collective-permute-done((bf16[4,128,256]{2,1,0:T(8,128)(2,1)S(1)}, bf16[4,128,256]{2,1,0:T(8,128)(2,1)S(1)}, u32[]{:S(2)}, u32[]{:S(2)}) %collective-permute-start.12) | collective-permute-done | bytes 262176 | tf_op jit(solution)/shard_map/ppermute | solution.py:295
  64.8 1.6 %collective-permute-start.22 = (bf16[4,128,256]{2,1,0:T(8,128)(2,1)S(1)}, bf16[4,128,256]{2,1,0:T(8,128)(2,1)S(1)}, u32[]{:S(2)}, u32[]{:S(2)}) collective-permute-start(bf16[4,128,256]{2,1,0:T(8,128)(2,1)S(1)} %collective-permute-done.14.refs_4_), channel_id=1, source_target_pairs={{8,0},{16,8},{24,16},{28,24},{20,28},{12,20},{4,12},{0,4},{9,1},{1... | collective-permute-start | bytes 786440 | tf_op jit(solution)/shard_map/ppermute | solution.py:295
  66.9 1.6 %collective-permute-start.21 = (bf16[256,512]{1,0:T(8,128)(2,1)S(1)}, bf16[256,512]{1,0:T(8,128)(2,1)S(1)}, u32[]{:S(2)}, u32[]{:S(2)}) collective-permute-start(bf16[256,512]{1,0:T(8,128)(2,1)S(1)} %fusion), channel_id=1, source_target_pairs={{0,2},{1,3},{2,0},{3,1},{4,6},{5,7},{6,4},{7,5},{8,10},{9,11},{10,... | collective-permute-start | bytes 786440 | tf_op jit(solution)/shard_map/ppermute | solution.py:356
  69.8 3.7 %collective-permute-done.22.refs_2_ = bf16[4,128,256]{2,1,0:T(8,128)(2,1)S(1)} collective-permute-done((bf16[4,128,256]{2,1,0:T(8,128)(2,1)S(1)}, bf16[4,128,256]{2,1,0:T(8,128)(2,1)S(1)}, u32[]{:S(2)}, u32[]{:S(2)}) %collective-permute-start.22) | collective-permute-done | bytes 262176 | tf_op jit(solution)/shard_map/ppermute | solution.py:295
  76.9 5.4 %collective-permute-done.24.refs_0_ = bf16[4,128,256]{2,1,0:T(8,128)(2,1)S(1)} collective-permute-done((bf16[4,128,256]{2,1,0:T(8,128)(2,1)S(1)}, bf16[4,128,256]{2,1,0:T(8,128)(2,1)S(1)}, u32[]{:S(2)}, u32[]{:S(2)}) %collective-permute-start.24) | collective-permute-done | bytes 262176 | tf_op jit(solution)/shard_map/ppermute | solution.py:295
  83.8 1.6 %collective-permute-start.27 = (bf16[4,128,256]{2,1,0:T(8,128)(2,1)S(1)}, bf16[4,128,256]{2,1,0:T(8,128)(2,1)S(1)}, u32[]{:S(2)}, u32[]{:S(2)}) collective-permute-start(bf16[4,128,256]{2,1,0:T(8,128)(2,1)S(1)} %collective-permute-done.22.refs_2_), channel_id=1, source_target_pairs={{8,0},{16,8},{24,16},{28,24},{20,28},{12,20},{4,12},{0,4},{9,1},{1... | collective-permute-start | bytes 786440 | tf_op jit(solution)/shard_map/ppermute | solution.py:295
  87.0 1.8 %collective-permute-start.29 = (bf16[4,128,256]{2,1,0:T(8,128)(2,1)S(1)}, bf16[4,128,256]{2,1,0:T(8,128)(2,1)S(1)}, u32[]{:S(2)}, u32[]{:S(2)}) collective-permute-start(bf16[4,128,256]{2,1,0:T(8,128)(2,1)S(1)} %collective-permute-done.24.refs_0_), channel_id=1, source_target_pairs={{8,0},{16,8},{24,16},{28,24},{20,28},{12,20},{4,12},{0,4},{9,1},{1... | collective-permute-start | bytes 786440 | tf_op jit(solution)/shard_map/ppermute | solution.py:295
  88.8 7.9 %orthonormal_first.1 = (f32[256,1024]{1,0:T(8,128)S(1)}, f32[256,256]{1,0:T(8,128)S(1)}) custom-call(s32[10]{0:T(128)S(1)} %pad_add_fusion.2.info, f32[256,512]{1,0:T(8,128)S(1)} %bitcast_subtract_fusion.1.mine, f32[256,512]{1,0:T(8,128)S(1)} %collective-permute-done.26.other), custom_call_target="tpu_custom_call" | custom-call | flops 8589934592 | bytes 2359296 | tf_op jit(solution)/shard_map/orthonormal_first/pallas_call | solution.py:264
  97.3 7.5 %orthonormal_last.1 = (bf16[256,1024]{1,0:T(8,128)(2,1)S(1)}, f32[256,256]{1,0:T(8,128)S(1)}) custom-call(s32[10]{0:T(128)S(1)} %pad_add_fusion.2.info, f32[256,1024]{1,0:T(8,128)S(1)} %get-tuple-element.126.y, f32[256,256]{1,0:T(8,128)S(1)} %get-tuple-element.128.begun), custom_call_target="tpu_custom_call" | custom-call | flops 8589934592 | bytes 2097152 | tf_op jit(solution)/shard_map/orthonormal_last/pallas_call | solution.py:264
  119.8 1.6 %copy-done.16 = bf16[1,4,1024,256]{3,2,1,0:T(8,128)(2,1)S(1)} copy-done((bf16[1,4,1024,256]{3,2,1,0:T(8,128)(2,1)S(1)}, bf16[1,4,1024,256]{3,2,1,0:T(8,128)(2,1)}, u32[]{:S(2)}) %copy-start.16) | copy-done | bytes 2097176
  122.5 2.9 %project.2 = (bf16[2,256,256]{2,1,0:T(8,128)(2,1)S(1)}, f32[2,256,256]{2,1,0:T(8,128)S(1)}) custom-call(s32[10]{0:T(128)S(1)} %pad_add_fusion.2.info, bf16[256,1024]{1,0:T(8,128)(2,1)S(1)} %copy-done.13, bf16[4,1024,256]{2,1,0:T(8,128)(2,1)S(1)} %bitcast.61, bf16[4,256,256]{2,1,0:T(8,128)(2,1)S(1)} %copy-done.20, ...), custom_call_target="tpu_custom_call" | custom-call | flops 2415919104 | bytes 6029312 | tf_op jit(solution)/shard_map/project/pallas_call | solution.py:264
  128.8 15.0 %orthonormal.1 = (bf16[256,1024]{1,0:T(8,128)(2,1)S(1)}, f32[256,256]{1,0:T(8,128)S(1)}) custom-call(s32[10]{0:T(128)S(1)} %pad_add_fusion.2.info, f32[256,512]{1,0:T(8,128)S(1)} %bitcast_subtract_fusion.mine, f32[256,512]{1,0:T(8,128)S(1)} %collective-permute-done.33.other), custom_call_target="tpu_custom_call" | custom-call | flops 17179869184 | bytes 1835008 | tf_op jit(solution)/shard_map/orthonormal/pallas_call | solution.py:264
  143.9 2.9 %project.3 = (bf16[2,256,256]{2,1,0:T(8,128)(2,1)S(1)}, f32[2,256,256]{2,1,0:T(8,128)S(1)}) custom-call(s32[10]{0:T(128)S(1)} %pad_add_fusion.2.info, bf16[256,1024]{1,0:T(8,128)(2,1)S(1)} %get-tuple-element.165.qt, bf16[4,1024,256]{2,1,0:T(8,128)(2,1)S(1)} %bitcast.62, bf16[4,256,256]{2,1,0:T(8,128)(2,1)S(1)} %copy-done.22, bf16[4,1024,256]{2,1,0:T(8,128)(2,1)S(1)} %copy-done.1), custom_call_target="tpu_custom_call" | custom-call | flops 2415919104 | bytes 6029312 | tf_op jit(solution)/shard_map/project/pallas_call | solution.py:264
  149.6 1.6 %collective-permute-start.37 = (bf16[256,256]{1,0:T(8,128)(2,1)S(1)}, bf16[256,256]{1,0:T(8,128)(2,1)S(1)}, u32[]{:S(2)}, u32[]{:S(2)}) collective-permute-start(bf16[256,256]{1,0:T(8,128)(2,1)S(1)} %fusion.5), channel_id=1, source_target_pairs={{0,2},{1,3},{2,0},{3,1},{4,6},{5,7},{6,4},{7,5},{8,10},{9,11},{10,... | collective-permute-start | bytes 393224 | tf_op jit(solution)/shard_map/ppermute | solution.py:356
  151.2 2.0 %collective-permute-done.35 = bf16[256,256]{1,0:T(8,128)(2,1)S(1)} collective-permute-done((bf16[256,256]{1,0:T(8,128)(2,1)S(1)}, bf16[256,256]{1,0:T(8,128)(2,1)S(1)}, u32[]{:S(2)}, u32[]{:S(2)}) %collective-permute-start.35) | collective-permute-done | bytes 131104 | tf_op jit(solution)/shard_map/ppermute | solution.py:356
  153.2 2.3 %collective-permute-done.37 = bf16[256,256]{1,0:T(8,128)(2,1)S(1)} collective-permute-done((bf16[256,256]{1,0:T(8,128)(2,1)S(1)}, bf16[256,256]{1,0:T(8,128)(2,1)S(1)}, u32[]{:S(2)}, u32[]{:S(2)}) %collective-permute-start.37) | collective-permute-done | bytes 131104 | tf_op jit(solution)/shard_map/ppermute | solution.py:356
  (139 shorter events, 53.2 us)
Async XLA Ops:
  1.9 10.2 %collective-permute-start.4 = (bf16[4,128,256]{2,1,0:T(8,128)(2,1)S(1)}, bf16[4,128,256]{2,1,0:T(8,128)(2,1)S(1)}, u32[]{:S(2)}, u32[]{:S(2)}) collective-permute-start(bf16[4,128,256]{2,1,0:T(8,128)(2,1)S(1)} %get-tuple-element.179.refs_0_), channel_id=1, source_target_pairs={{8,0},{16,8},{24,16},{28,24},{20,28},{12,20},{4,12},{0,4},{9,1},{1... | collective-permute-start | bytes 786440 | tf_op jit(solution)/shard_map/ppermute | solution.py:295
  4.8 9.2 %collective-permute-start.5 = (bf16[4,128,256]{2,1,0:T(8,128)(2,1)S(1)}, bf16[4,128,256]{2,1,0:T(8,128)(2,1)S(1)}, u32[]{:S(2)}, u32[]{:S(2)}) collective-permute-start(bf16[4,128,256]{2,1,0:T(8,128)(2,1)S(1)} %get-tuple-element.179.refs_0_), channel_id=1, source_target_pairs={{0,8},{8,16},{16,24},{24,28},{28,20},{20,12},{12,4},{4,0},{1,9},{9... | collective-permute-start | bytes 786440 | tf_op jit(solution)/shard_map/ppermute | solution.py:298
  6.8 11.0 %collective-permute-start = (bf16[4,128,256]{2,1,0:T(8,128)(2,1)S(1)}, bf16[4,128,256]{2,1,0:T(8,128)(2,1)}, u32[]{:S(2)}, u32[]{:S(2)}) collective-permute-start(bf16[4,128,256]{2,1,0:T(8,128)(2,1)S(1)} %get-tuple-element.177.refs_3_), channel_id=1, source_target_pairs={{8,0},{16,8},{24,16},{28,24},{20,28},{12,20},{4,12},{0,4},{9,1},{1... | collective-permute-start | bytes 786440 | tf_op jit(solution)/shard_map/ppermute | solution.py:295
  8.6 11.2 %collective-permute-start.2 = (bf16[4,128,256]{2,1,0:T(8,128)(2,1)S(1)}, bf16[4,128,256]{2,1,0:T(8,128)(2,1)}, u32[]{:S(2)}, u32[]{:S(2)}) collective-permute-start(bf16[4,128,256]{2,1,0:T(8,128)(2,1)S(1)} %get-tuple-element.177.refs_3_), channel_id=1, source_target_pairs={{0,8},{8,16},{16,24},{24,28},{28,20},{20,12},{12,4},{4,0},{1,9},{9... | collective-permute-start | bytes 786440 | tf_op jit(solution)/shard_map/ppermute | solution.py:298
  12.1 11.2 %collective-permute-start.6 = (bf16[4,128,256]{2,1,0:T(8,128)(2,1)S(1)}, bf16[4,128,256]{2,1,0:T(8,128)(2,1)S(1)}, u32[]{:S(2)}, u32[]{:S(2)}) collective-permute-start(bf16[4,128,256]{2,1,0:T(8,128)(2,1)S(1)} %collective-permute-done.4.refs_1_), channel_id=1, source_target_pairs={{8,0},{16,8},{24,16},{28,24},{20,28},{12,20},{4,12},{0,4},{9,1},{1... | collective-permute-start | bytes 786440 | tf_op jit(solution)/shard_map/ppermute | solution.py:295
  14.1 11.2 %collective-permute-start.7 = (bf16[4,128,256]{2,1,0:T(8,128)(2,1)S(1)}, bf16[4,128,256]{2,1,0:T(8,128)(2,1)S(1)}, u32[]{:S(2)}, u32[]{:S(2)}) collective-permute-start(bf16[4,128,256]{2,1,0:T(8,128)(2,1)S(1)} %collective-permute-done.5.refs_2_), channel_id=1, source_target_pairs={{0,8},{8,16},{16,24},{24,28},{28,20},{20,12},{12,4},{4,0},{1,9},{9... | collective-permute-start | bytes 786440 | tf_op jit(solution)/shard_map/ppermute | solution.py:298
  17.8 11.2 %collective-permute-start.1 = (bf16[4,128,256]{2,1,0:T(8,128)(2,1)}, bf16[4,128,256]{2,1,0:T(8,128)(2,1)S(1)}, u32[]{:S(2)}, u32[]{:S(2)}) collective-permute-start(bf16[4,128,256]{2,1,0:T(8,128)(2,1)} %collective-permute-done.refs_4_), channel_id=1, source_target_pairs={{8,0},{16,8},{24,16},{28,24},{20,28},{12,20},{4,12},{0,4},{9,1},{1... | collective-permute-start | bytes 786440 | tf_op jit(solution)/shard_map/ppermute | solution.py:295
  19.8 11.1 %collective-permute-start.3 = (bf16[4,128,256]{2,1,0:T(8,128)(2,1)}, bf16[4,128,256]{2,1,0:T(8,128)(2,1)S(1)}, u32[]{:S(2)}, u32[]{:S(2)}) collective-permute-start(bf16[4,128,256]{2,1,0:T(8,128)(2,1)} %collective-permute-done.2.refs_5_), channel_id=1, source_target_pairs={{0,8},{8,16},{16,24},{24,28},{28,20},{20,12},{12,4},{4,0},{1,9},{9... | collective-permute-start | bytes 786440 | tf_op jit(solution)/shard_map/ppermute | solution.py:298
  25.3 9.2 %collective-permute-start.8 = (bf16[4,128,256]{2,1,0:T(8,128)(2,1)S(1)}, bf16[4,128,256]{2,1,0:T(8,128)(2,1)S(1)}, u32[]{:S(2)}, u32[]{:S(2)}) collective-permute-start(bf16[4,128,256]{2,1,0:T(8,128)(2,1)S(1)} %collective-permute-done.6.refs_0_), channel_id=1, source_target_pairs={{8,0},{16,8},{24,16},{28,24},{20,28},{12,20},{4,12},{0,4},{9,1},{1... | collective-permute-start | bytes 786440 | tf_op jit(solution)/shard_map/ppermute | solution.py:295
  26.9 9.7 %collective-permute-start.9 = (bf16[4,128,256]{2,1,0:T(8,128)(2,1)S(1)}, bf16[4,128,256]{2,1,0:T(8,128)(2,1)S(1)}, u32[]{:S(2)}, u32[]{:S(2)}) collective-permute-start(bf16[4,128,256]{2,1,0:T(8,128)(2,1)S(1)} %collective-permute-done.7.refs_1_), channel_id=1, source_target_pairs={{0,8},{8,16},{16,24},{24,28},{28,20},{20,12},{12,4},{4,0},{1,9},{9... | collective-permute-start | bytes 786440 | tf_op jit(solution)/shard_map/ppermute | solution.py:298
  30.9 11.2 %collective-permute-start.13 = (bf16[4,128,256]{2,1,0:T(8,128)(2,1)S(1)}, bf16[4,128,256]{2,1,0:T(8,128)(2,1)S(1)}, u32[]{:S(2)}, u32[]{:S(2)}) collective-permute-start(bf16[4,128,256]{2,1,0:T(8,128)(2,1)S(1)} %collective-permute-done.3.refs_3_), channel_id=1, source_target_pairs={{0,8},{8,16},{16,24},{24,28},{28,20},{20,12},{12,4},{4,0},{1,9},{9... | collective-permute-start | bytes 786440 | tf_op jit(solution)/shard_map/ppermute | solution.py:298
  31.0 12.7 %collective-permute-start.14 = (bf16[4,128,256]{2,1,0:T(8,128)(2,1)S(1)}, bf16[4,128,256]{2,1,0:T(8,128)(2,1)S(1)}, u32[]{:S(2)}, u32[]{:S(2)}) collective-permute-start(bf16[4,128,256]{2,1,0:T(8,128)(2,1)S(1)} %copy-done.10), channel_id=1, source_target_pairs={{8,0},{16,8},{24,16},{28,24},{20,28},{12,20},{4,12},{0,4},{9,1},{1... | collective-permute-start | bytes 786440 | tf_op jit(solution)/shard_map/ppermute | solution.py:295
  33.0 14.8 %collective-permute-start.15 = (bf16[4,128,256]{2,1,0:T(8,128)(2,1)S(1)}, bf16[4,128,256]{2,1,0:T(8,128)(2,1)S(1)}, u32[]{:S(2)}, u32[]{:S(2)}) collective-permute-start(bf16[4,128,256]{2,1,0:T(8,128)(2,1)S(1)} %copy-done.10), channel_id=1, source_target_pairs={{0,8},{8,16},{16,24},{24,28},{28,20},{20,12},{12,4},{4,0},{1,9},{9... | collective-permute-start | bytes 786440 | tf_op jit(solution)/shard_map/ppermute | solution.py:298
  34.5 13.4 %collective-permute-start.10 = (bf16[4,128,256]{2,1,0:T(8,128)(2,1)S(1)}, bf16[4,128,256]{2,1,0:T(8,128)(2,1)S(1)}, u32[]{:S(2)}, u32[]{:S(2)}) collective-permute-start(bf16[4,128,256]{2,1,0:T(8,128)(2,1)S(1)} %get-tuple-element.99.refs_0_), channel_id=1, source_target_pairs={{8,0},{16,8},{24,16},{28,24},{20,28},{12,20},{4,12},{0,4},{9,1},{1... | collective-permute-start | bytes 786440 | tf_op jit(solution)/shard_map/ppermute | solution.py:295
  36.5 16.9 %collective-permute-start.11 = (bf16[4,128,256]{2,1,0:T(8,128)(2,1)S(1)}, bf16[4,128,256]{2,1,0:T(8,128)(2,1)S(1)}, u32[]{:S(2)}, u32[]{:S(2)}) collective-permute-start(bf16[4,128,256]{2,1,0:T(8,128)(2,1)S(1)} %get-tuple-element.99.refs_0_), channel_id=1, source_target_pairs={{0,8},{8,16},{16,24},{24,28},{28,20},{20,12},{12,4},{4,0},{1,9},{9... | collective-permute-start | bytes 786440 | tf_op jit(solution)/shard_map/ppermute | solution.py:298
  42.2 14.9 %collective-permute-start.17 = (bf16[4,128,256]{2,1,0:T(8,128)(2,1)S(1)}, bf16[4,128,256]{2,1,0:T(8,128)(2,1)S(1)}, u32[]{:S(2)}, u32[]{:S(2)}) collective-permute-start(bf16[4,128,256]{2,1,0:T(8,128)(2,1)S(1)} %collective-permute-done.1.refs_2_), channel_id=1, source_target_pairs={{8,0},{16,8},{24,16},{28,24},{20,28},{12,20},{4,12},{0,4},{9,1},{1... | collective-permute-start | bytes 786440 | tf_op jit(solution)/shard_map/ppermute | solution.py:295
  47.8 11.2 %collective-permute-start.16 = (bf16[4,128,256]{2,1,0:T(8,128)(2,1)S(1)}, bf16[4,128,256]{2,1,0:T(8,128)(2,1)S(1)}, u32[]{:S(2)}, u32[]{:S(2)}) collective-permute-start(bf16[4,128,256]{2,1,0:T(8,128)(2,1)S(1)} %collective-permute-done.13.refs_3_), channel_id=1, source_target_pairs={{0,8},{8,16},{16,24},{24,28},{28,20},{20,12},{12,4},{4,0},{1,9},{9... | collective-permute-start | bytes 786440 | tf_op jit(solution)/shard_map/ppermute | solution.py:298
  53.4 8.2 %collective-permute-start.12 = (bf16[4,128,256]{2,1,0:T(8,128)(2,1)S(1)}, bf16[4,128,256]{2,1,0:T(8,128)(2,1)S(1)}, u32[]{:S(2)}, u32[]{:S(2)}) collective-permute-start(bf16[4,128,256]{2,1,0:T(8,128)(2,1)S(1)} %collective-permute-done.8.refs_0_), channel_id=1, source_target_pairs={{8,0},{16,8},{24,16},{28,24},{20,28},{12,20},{4,12},{0,4},{9,1},{1... | collective-permute-start | bytes 786440 | tf_op jit(solution)/shard_map/ppermute | solution.py:295
  55.0 9.7 %collective-permute-start.18 = (bf16[4,128,256]{2,1,0:T(8,128)(2,1)S(1)}, bf16[4,128,256]{2,1,0:T(8,128)(2,1)S(1)}, u32[]{:S(2)}, u32[]{:S(2)}) collective-permute-start(bf16[4,128,256]{2,1,0:T(8,128)(2,1)S(1)} %collective-permute-done.10.refs_1_), channel_id=1, source_target_pairs={{8,0},{16,8},{24,16},{28,24},{20,28},{12,20},{4,12},{0,4},{9,1},{1... | collective-permute-start | bytes 786440 | tf_op jit(solution)/shard_map/ppermute | solution.py:295
  56.6 8.1 %collective-permute-start.19 = (bf16[4,128,256]{2,1,0:T(8,128)(2,1)S(1)}, bf16[4,128,256]{2,1,0:T(8,128)(2,1)S(1)}, u32[]{:S(2)}, u32[]{:S(2)}) collective-permute-start(bf16[4,128,256]{2,1,0:T(8,128)(2,1)S(1)} %collective-permute-done.11.refs_2_), channel_id=1, source_target_pairs={{0,8},{8,16},{16,24},{24,28},{28,20},{20,12},{12,4},{4,0},{1,9},{9... | collective-permute-start | bytes 786440 | tf_op jit(solution)/shard_map/ppermute | solution.py:298
  64.8 8.7 %collective-permute-start.22 = (bf16[4,128,256]{2,1,0:T(8,128)(2,1)S(1)}, bf16[4,128,256]{2,1,0:T(8,128)(2,1)S(1)}, u32[]{:S(2)}, u32[]{:S(2)}) collective-permute-start(bf16[4,128,256]{2,1,0:T(8,128)(2,1)S(1)} %collective-permute-done.14.refs_4_), channel_id=1, source_target_pairs={{8,0},{16,8},{24,16},{28,24},{20,28},{12,20},{4,12},{0,4},{9,1},{1... | collective-permute-start | bytes 786440 | tf_op jit(solution)/shard_map/ppermute | solution.py:295
  66.4 8.4 %collective-permute-start.23 = (bf16[4,128,256]{2,1,0:T(8,128)(2,1)S(1)}, bf16[4,128,256]{2,1,0:T(8,128)(2,1)S(1)}, u32[]{:S(2)}, u32[]{:S(2)}) collective-permute-start(bf16[4,128,256]{2,1,0:T(8,128)(2,1)S(1)} %collective-permute-done.15.refs_5_), channel_id=1, source_target_pairs={{0,8},{8,16},{16,24},{24,28},{28,20},{20,12},{12,4},{4,0},{1,9},{9... | collective-permute-start | bytes 786440 | tf_op jit(solution)/shard_map/ppermute | solution.py:298
  66.9 9.9 %collective-permute-start.21 = (bf16[256,512]{1,0:T(8,128)(2,1)S(1)}, bf16[256,512]{1,0:T(8,128)(2,1)S(1)}, u32[]{:S(2)}, u32[]{:S(2)}) collective-permute-start(bf16[256,512]{1,0:T(8,128)(2,1)S(1)} %fusion), channel_id=1, source_target_pairs={{0,2},{1,3},{2,0},{3,1},{4,6},{5,7},{6,4},{7,5},{8,10},{9,11},{10,... | collective-permute-start | bytes 786440 | tf_op jit(solution)/shard_map/ppermute | solution.py:356
  74.8 7.5 %collective-permute-start.24 = (bf16[4,128,256]{2,1,0:T(8,128)(2,1)S(1)}, bf16[4,128,256]{2,1,0:T(8,128)(2,1)S(1)}, u32[]{:S(2)}, u32[]{:S(2)}) collective-permute-start(bf16[4,128,256]{2,1,0:T(8,128)(2,1)S(1)} %collective-permute-done.18.refs_0_), channel_id=1, source_target_pairs={{8,0},{16,8},{24,16},{28,24},{20,28},{12,20},{4,12},{0,4},{9,1},{1... | collective-permute-start | bytes 786440 | tf_op jit(solution)/shard_map/ppermute | solution.py:295
  76.3 7.3 %collective-permute-start.25 = (bf16[4,128,256]{2,1,0:T(8,128)(2,1)S(1)}, bf16[4,128,256]{2,1,0:T(8,128)(2,1)S(1)}, u32[]{:S(2)}, u32[]{:S(2)}) collective-permute-start(bf16[4,128,256]{2,1,0:T(8,128)(2,1)S(1)} %collective-permute-done.19.refs_1_), channel_id=1, source_target_pairs={{0,8},{8,16},{16,24},{24,28},{28,20},{20,12},{12,4},{4,0},{1,9},{9... | collective-permute-start | bytes 786440 | tf_op jit(solution)/shard_map/ppermute | solution.py:298
  83.8 13.0 %collective-permute-start.27 = (bf16[4,128,256]{2,1,0:T(8,128)(2,1)S(1)}, bf16[4,128,256]{2,1,0:T(8,128)(2,1)S(1)}, u32[]{:S(2)}, u32[]{:S(2)}) collective-permute-start(bf16[4,128,256]{2,1,0:T(8,128)(2,1)S(1)} %collective-permute-done.22.refs_2_), channel_id=1, source_target_pairs={{8,0},{16,8},{24,16},{28,24},{20,28},{12,20},{4,12},{0,4},{9,1},{1... | collective-permute-start | bytes 786440 | tf_op jit(solution)/shard_map/ppermute | solution.py:295
  85.4 11.3 %collective-permute-start.28 = (bf16[4,128,256]{2,1,0:T(8,128)(2,1)S(1)}, bf16[4,128,256]{2,1,0:T(8,128)(2,1)S(1)}, u32[]{:S(2)}, u32[]{:S(2)}) collective-permute-start(bf16[4,128,256]{2,1,0:T(8,128)(2,1)S(1)} %collective-permute-done.23.refs_3_), channel_id=1, source_target_pairs={{0,8},{8,16},{16,24},{24,28},{28,20},{20,12},{12,4},{4,0},{1,9},{9... | collective-permute-start | bytes 786440 | tf_op jit(solution)/shard_map/ppermute | solution.py:298
  87.0 19.7 %collective-permute-start.29 = (bf16[4,128,256]{2,1,0:T(8,128)(2,1)S(1)}, bf16[4,128,256]{2,1,0:T(8,128)(2,1)S(1)}, u32[]{:S(2)}, u32[]{:S(2)}) collective-permute-start(bf16[4,128,256]{2,1,0:T(8,128)(2,1)S(1)} %collective-permute-done.24.refs_0_), channel_id=1, source_target_pairs={{8,0},{16,8},{24,16},{28,24},{20,28},{12,20},{4,12},{0,4},{9,1},{1... | collective-permute-start | bytes 786440 | tf_op jit(solution)/shard_map/ppermute | solution.py:295
  96.8 10.0 %collective-permute-start.30 = (bf16[4,128,256]{2,1,0:T(8,128)(2,1)S(1)}, bf16[4,128,256]{2,1,0:T(8,128)(2,1)S(1)}, u32[]{:S(2)}, u32[]{:S(2)}) collective-permute-start(bf16[4,128,256]{2,1,0:T(8,128)(2,1)S(1)} %collective-permute-done.28.refs_3_), channel_id=1, source_target_pairs={{0,8},{8,16},{16,24},{24,28},{28,20},{20,12},{12,4},{4,0},{1,9},{9... | collective-permute-start | bytes 786440 | tf_op jit(solution)/shard_map/ppermute | solution.py:298
  111.7 13.6 %collective-permute-start.32 = (bf16[256,512]{1,0:T(8,128)(2,1)}, bf16[256,512]{1,0:T(8,128)(2,1)}, u32[]{:S(2)}, u32[]{:S(2)}) collective-permute-start(bf16[256,512]{1,0:T(8,128)(2,1)} %fusion.1), channel_id=1, source_target_pairs={{0,2},{1,3},{2,0},{3,1},{4,6},{5,7},{6,4},{7,5},{8,10},{9,11},{10,... | collective-permute-start | bytes 786440 | tf_op jit(solution)/shard_map/ppermute | solution.py:356
  147.1 6.1 %collective-permute-start.35 = (bf16[256,256]{1,0:T(8,128)(2,1)S(1)}, bf16[256,256]{1,0:T(8,128)(2,1)S(1)}, u32[]{:S(2)}, u32[]{:S(2)}) collective-permute-start(bf16[256,256]{1,0:T(8,128)(2,1)S(1)} %fusion.4), channel_id=1, source_target_pairs={{0,2},{1,3},{2,0},{3,1},{4,6},{5,7},{6,4},{7,5},{8,10},{9,11},{10,... | collective-permute-start | bytes 393224 | tf_op jit(solution)/shard_map/ppermute | solution.py:356
  149.6 5.9 %collective-permute-start.37 = (bf16[256,256]{1,0:T(8,128)(2,1)S(1)}, bf16[256,256]{1,0:T(8,128)(2,1)S(1)}, u32[]{:S(2)}, u32[]{:S(2)}) collective-permute-start(bf16[256,256]{1,0:T(8,128)(2,1)S(1)} %fusion.5), channel_id=1, source_target_pairs={{0,2},{1,3},{2,0},{3,1},{4,6},{5,7},{6,4},{7,5},{8,10},{9,11},{10,... | collective-permute-start | bytes 393224 | tf_op jit(solution)/shard_map/ppermute | solution.py:356
  (33 other events, 173.8 us)

commit v2 on v1

--- a/solution.py
+++ b/solution.py
@@ -212,11 +212,16 @@
         out[...] = total.astype(out.dtype)
 
 
-def project_kernel(blocks, info, qt, panel_u, cross, u_all, give, keep, work):
+def project_kernel(blocks, c, info, qt, panel_u, cross, u_all, orig_u, orig_v, give, keep, own, work, u_buf, v_buf, sems):
     priors, order, width = u_all.shape
     slab = order // blocks
     pairs, share, _ = keep.shape
     core = info[0]
+    fetch_u = pltpu.make_async_copy(orig_u.at[c], u_buf, sems.at[0])
+    rows = pl.ds(pl.multiple_of(info[1] * share, 16), share)
+    fetch_v = pltpu.make_async_copy(orig_v.at[c, rows], v_buf, sems.at[1])
+    fetch_u.start()
+    fetch_v.start()
     mids = []
     for j in range(priors):
         inner = dot(qt[...], panel_u[j]).astype(BF16)
@@ -233,13 +238,9 @@
         for out, which in ((give, 1 - core), (keep, core)):
             rows = pl.ds(pl.multiple_of((2 * a + which) * share, SUB), share)
             out[a] = work[rows, :].astype(out.dtype)
-
-
-def left_kernel(info, qt, orig_u, orig_v, out):
-    share = out.shape[0]
-    left = dot(qt[...], orig_u[...]).astype(BF16)
-    rows = orig_v[pl.ds(pl.multiple_of(info[1] * share, SUB), share), :]
-    out[...] = dot11(rows, left)
+    fetch_u.wait()
+    fetch_v.wait()
+    own[...] = dot11(v_buf[...], dot(qt[...], u_buf[...]).astype(BF16))
 
 
 def turn_kernel(panel_v, sampler, panel_vt, sampler_t):
@@ -256,7 +257,7 @@
         out[c] = dot11(proj, orig_u[c, rows, :])
 
 
-def run(kernel, scalars, arrays, outs, scratch, limit, flops, name, aliases={}):
+def run(kernel, scalars, arrays, outs, scratch, limit, flops, name, aliases={}, apart=()):
     smem = pl.BlockSpec(memory_space=pltpu.SMEM)
     vmem = pl.BlockSpec(memory_space=pltpu.VMEM)
     shapes = [jax.ShapeDtypeStruct(*o) for o in outs]
@@ -264,14 +265,14 @@
     return pl.pallas_call(
         kernel,
         out_shape=shapes,
-        in_specs=[smem] * len(scalars) + [vmem] * len(arrays),
+        in_specs=[smem] * len(scalars) + [vmem] * len(arrays) + [pl.BlockSpec(memory_space=pl.ANY)] * len(apart),
         out_specs=[vmem] * len(shapes),
         scratch_shapes=scratch,
         input_output_aliases=aliases,
         compiler_params=pltpu.CompilerParams(vmem_limit_bytes=limit * MIB),
         cost_estimate=pl.CostEstimate(flops=flops, bytes_accessed=moved, transcendentals=0),
         name=name,
-    )(*scalars, *arrays)
+    )(*scalars, *arrays, *apart)
 
 
 def ring_order(count):
@@ -387,7 +388,7 @@
         for shift in range(1, pairs):
             chip = chip + shifted(sent, shift).astype(F32)
         if beside is not None:
-            chip = beside.hold(beside.hold(chip, 1, 2), 0, 3)
+            chip = beside.hold(beside.hold(chip, 0, 2), 1, 3)
         chip, *outs = lax.optimization_barrier((chip, *outs))
         ymine = start[c] - chip
         yother = lax.ppermute(ymine, "cols", swap)
@@ -396,16 +397,15 @@
     finals = [((width, order), BF16), ((share, width), F32)]
 
     def projected(c, blocks, qt, cross, u_all):
-        give, keep = run(
-            functools.partial(project_kernel, blocks), [info], [qt, panel_u, cross, u_all],
-            [((pairs, share, width), BF16), ((pairs, share, width), F32)],
-            [pltpu.VMEM((order, width), F32)], 16, 2 * priors * square * (2 * order + width), "project"
+        return run(
+            functools.partial(project_kernel, blocks, c), [info], [qt, panel_u, cross, u_all],
+            [((pairs, share, width), BF16), ((pairs, share, width), F32), ((share, width), F32)],
+            [
+                pltpu.VMEM((order, width), F32), pltpu.VMEM((order, width), BF16), pltpu.VMEM((share, width), BF16),
+                pltpu.SemaphoreType.DMA((2,))
+            ],
+            16, 2 * priors * square * (2 * order + width), "project", apart=[orig_u, orig_v]
         )
-        (own,) = run(
-            left_kernel, [info], [qt, orig_u[c], orig_v[c]], [((share, width), F32)], [], 8,
-            square * (order + share), "left"
-        )
-        return give, keep, own
 
     def halved(give, keep, own):
         chip = keep + lax.ppermute(give, "cols", swap).astype(F32)
@@ -447,7 +447,7 @@
                         [now.hold(pivot_u[c + 1], 0, last - 2), now.hold(pivot_v[c + 1], 1, last - 2)], ring, "rows"
                     )
                     later.step(1)
-                    now.up[0] = later.hold(now.up[0], 0, 1)
+                    now.up[0] = later.hold(now.up[0], 1, 1)
                     now.down[1] = later.hold(now.down[1], 1, 1)
                 now.step(number)
                 if c == 0 and number < last:
@@ -465,8 +465,8 @@
             if later is not None:
                 kept = list(taken(later, 1, kept))
                 later.step(2)
-                give = later.tie(give, 2, (0,))
-                kept[0] = later.tie(kept[0], 2, (1,))
+                give = later.hold(later.hold(give, 0, 1), 1, 2)
+                kept[0] = later.tie(kept[0], 2, (0,))
                 later.step(3)
                 kept = list(taken(later, 2, kept))
             outs = projected(c - 1, count, *parts) if parts is not None and later is None else ()
@@ -482,7 +482,7 @@
                     first_kernel, [info], [ymine, yother], [((width, order), F32), ((width, width), F32)], [matrix], 12,
                     64 * square * order, "orthonormal_first"
                 )
-                work = later.tie(work, 3, (1,))
+                work = later.tie(work, 3, (0,))
                 kept[0] = later.tie(kept[0], 3, (0,))
                 qt, rows = run(
                     last_kernel, [info], [yt, work], finals, [tall, matrix], 12, 64 * square * order, "orthonormal_last"

time: 157 us -> 158 us (level)
    ppermute x14, starting transfers between devices: 3.74 us -> 25.1 us  [step(): self.down[t] = lax.ppermute(self.down[t], self.axis, self.behind)]
    ppermute x14, starting transfers between devices: 25.6 us -> 5.71 us  [step(): self.up[t] = lax.ppermute(self.up[t], self.axis, self.ahead)]
    ppermute x14, waiting for transfers between devices: 18.9 us -> 7.62 us  [step(): self.up[t] = lax.ppermute(self.up[t], self.axis, self.ahead)]
    ppermute x14, waiting for transfers between devices: 21.4 us -> 31.3 us  [step(): self.down[t] = lax.ppermute(self.down[t], self.axis, self.behind)]
    unnamed x54, local copies, waits for them, and re-layouts: 9.26 us -> 11.5 us
    pallas_call x19 -> x17, Pallas kernels: 53.4 us -> 53.3 us  [run(): pl.pallas_call(kernel, out_shape=shapes, in_specs=[smem] * len(scalars) +...]
  transfers between devices with their start and end apart: 38 -> 38, of which waited for: 20 -> 20; matrix products, arithmetic and copies ran while one was open for 3% -> 2% of each run, Pallas kernels for 21% -> 20%
where the time goes in v2:
time: 158 us; the launch traced here: 157 us
  Pallas kernels  53.3 us (34%)
  waiting for transfers between devices  47.3 us (30%)
  starting transfers between devices  37.2 us (24%)
  local copies, waits for them, and re-layouts  14.4 us (9%)
  other arithmetic  4.17 us (3%)
    pallas_call x17, Pallas kernels, run(): pl.pallas_call(kernel, out_shape=shapes, in_specs=[smem] * len(scalars) +...  53.3 us
    ppermute x14, waiting for transfers between devices, step(): self.down[t] = lax.ppermute(self.down[t], self.axis, self.behind)  31.3 us
    ppermute x14, starting transfers between devices, step(): self.down[t] = lax.ppermute(self.down[t], self.axis, self.behind)  25.1 us
    unnamed x54, local copies, waits for them, and re-layouts  11.5 us
    ppermute x14, waiting for transfers between devices, step(): self.up[t] = lax.ppermute(self.up[t], self.axis, self.ahead)  7.62 us
    ppermute x14, starting transfers between devices, step(): self.up[t] = lax.ppermute(self.up[t], self.axis, self.ahead)  5.71 us
    ppermute x4, waiting for transfers between devices, shifted(): lax.ppermute(x, 'cols', [(i, (i + 2 * shift) % cols) for i in range(cols)])  5.4 us
    ppermute x4, starting transfers between devices, shifted(): lax.ppermute(x, 'cols', [(i, (i + 2 * shift) % cols) for i in range(cols)])  5.19 us
  transfers between devices with their start and end apart: 38, of which 20 were waited for; matrix products, arithmetic and copies ran while one was open for 2% of the time, Pallas kernels for 20%

profile of v2, /device:TPU:0, one launch (start us, length us, event | category | flops | bytes accessed | tf_op | source)
XLA Modules:
  0.0 157.4 jit_solution(8417074823228986014)
XLA Ops:
  1.8 3.1 %collective-permute-start.5 = (bf16[4,128,256]{2,1,0:T(8,128)(2,1)S(1)}, bf16[4,128,256]{2,1,0:T(8,128)(2,1)S(1)}, u32[]{:S(2)}, u32[]{:S(2)}) collective-permute-start(bf16[4,128,256]{2,1,0:T(8,128)(2,1)S(1)} %get-tuple-element.184.refs_0_), channel_id=1, source_target_pairs={{0,8},{8,16},{16,24},{24,28},{28,20},{20,12},{12,4},{4,0},{1,9},{9... | collective-permute-start | bytes 786440 | tf_op jit(solution)/shard_map/ppermute | solution.py:299
  5.9 2.1 %collective-permute-start.2 = (bf16[4,128,256]{2,1,0:T(8,128)(2,1)S(1)}, bf16[4,128,256]{2,1,0:T(8,128)(2,1)}, u32[]{:S(2)}, u32[]{:S(2)}) collective-permute-start(bf16[4,128,256]{2,1,0:T(8,128)(2,1)S(1)} %get-tuple-element.183.refs_3_), channel_id=1, source_target_pairs={{0,8},{8,16},{16,24},{24,28},{28,20},{20,12},{12,4},{4,0},{1,9},{9... | collective-permute-start | bytes 786440 | tf_op jit(solution)/shard_map/ppermute | solution.py:299
  8.7 3.2 %collective-permute-done.5.refs_2_ = bf16[4,128,256]{2,1,0:T(8,128)(2,1)S(1)} collective-permute-done((bf16[4,128,256]{2,1,0:T(8,128)(2,1)S(1)}, bf16[4,128,256]{2,1,0:T(8,128)(2,1)S(1)}, u32[]{:S(2)}, u32[]{:S(2)}) %collective-permute-start.5) | collective-permute-done | bytes 262176 | tf_op jit(solution)/shard_map/ppermute | solution.py:299
  11.9 2.1 %collective-permute-start.7 = (bf16[4,128,256]{2,1,0:T(8,128)(2,1)S(1)}, bf16[4,128,256]{2,1,0:T(8,128)(2,1)S(1)}, u32[]{:S(2)}, u32[]{:S(2)}) collective-permute-start(bf16[4,128,256]{2,1,0:T(8,128)(2,1)S(1)} %collective-permute-done.5.refs_2_), channel_id=1, source_target_pairs={{0,8},{8,16},{16,24},{24,28},{28,20},{20,12},{12,4},{4,0},{1,9},{9... | collective-permute-start | bytes 786440 | tf_op jit(solution)/shard_map/ppermute | solution.py:299
  14.2 3.4 %collective-permute-done.2.refs_5_ = bf16[4,128,256]{2,1,0:T(8,128)(2,1)} collective-permute-done((bf16[4,128,256]{2,1,0:T(8,128)(2,1)S(1)}, bf16[4,128,256]{2,1,0:T(8,128)(2,1)}, u32[]{:S(2)}, u32[]{:S(2)}) %collective-permute-start.2) | collective-permute-done | bytes 262176 | tf_op jit(solution)/shard_map/ppermute | solution.py:299
  17.6 2.1 %collective-permute-start.3 = (bf16[4,128,256]{2,1,0:T(8,128)(2,1)}, bf16[4,128,256]{2,1,0:T(8,128)(2,1)S(1)}, u32[]{:S(2)}, u32[]{:S(2)}) collective-permute-start(bf16[4,128,256]{2,1,0:T(8,128)(2,1)} %collective-permute-done.2.refs_5_), channel_id=1, source_target_pairs={{0,8},{8,16},{16,24},{24,28},{28,20},{20,12},{12,4},{4,0},{1,9},{9... | collective-permute-start | bytes 786440 | tf_op jit(solution)/shard_map/ppermute | solution.py:299
  19.9 1.6 %copy-done.12 = bf16[1,4,1024,256]{3,2,1,0:T(8,128)(2,1)S(1)} copy-done((bf16[1,4,1024,256]{3,2,1,0:T(8,128)(2,1)S(1)}, bf16[1,4,1024,256]{3,2,1,0:T(8,128)(2,1)}, u32[]{:S(2)}) %copy-start.12) | copy-done | bytes 2097176
  23.0 1.6 %start.1 = f32[2,256,512]{2,1,0:T(8,128)S(1)} custom-call(s32[10]{0:T(128)S(1)} %pad_add_fusion.2.info, bf16[256,1024]{1,0:T(8,128)(2,1)S(1)} %get-tuple-element.91.sampler_t, bf16[2,1024,256]{2,1,0:T(8,128)(2,1)S(1)} %bitcast.46, bf16[2,1024,256]{2,1,0:T(8,128)(2,1)S(1)} %bitcast.49), custom_call_target="tpu_custom_call" | custom-call | flops 402653184 | bytes 3670016 | tf_op jit(solution)/shard_map/start/pallas_call | solution.py:265
  24.6 1.8 %gather.8 = (f32[4,256,256]{2,1,0:T(8,128)S(1)}, f32[4,256,256]{2,1,0:T(8,128)S(1)}, bf16[4,1024,256]{2,1,0:T(8,128)(2,1)S(1)}) custom-call(s32[10]{0:T(128)S(1)} %pad_add_fusion.2.info, bf16[4,256,1024]{2,1,0:T(8,128)(2,1)S(1)} %get-tuple-element.93.panel_vt, bf16[256,1024]{1,0:T(8,128)(2,1)S(1)} %get-tuple-element.91.sampler_t, ...), custom_call_target="tpu_custom_call" | custom-call | flops 402653184 | bytes 8388608 | tf_op jit(solution)/shard_map/gather/pallas_call | solution.py:265
  29.8 1.7 %collective-permute-start.9 = (bf16[4,128,256]{2,1,0:T(8,128)(2,1)S(1)}, bf16[4,128,256]{2,1,0:T(8,128)(2,1)S(1)}, u32[]{:S(2)}, u32[]{:S(2)}) collective-permute-start(bf16[4,128,256]{2,1,0:T(8,128)(2,1)S(1)} %collective-permute-done.7.refs_1_), channel_id=1, source_target_pairs={{0,8},{8,16},{16,24},{24,28},{28,20},{20,12},{12,4},{4,0},{1,9},{9... | collective-permute-start | bytes 786440 | tf_op jit(solution)/shard_map/ppermute | solution.py:299
  31.5 1.6 %collective-permute-start.11 = (bf16[4,128,256]{2,1,0:T(8,128)(2,1)S(1)}, bf16[4,128,256]{2,1,0:T(8,128)(2,1)S(1)}, u32[]{:S(2)}, u32[]{:S(2)}) collective-permute-start(bf16[4,128,256]{2,1,0:T(8,128)(2,1)S(1)} %get-tuple-element.104.refs_3_), channel_id=1, source_target_pairs={{0,8},{8,16},{16,24},{24,28},{28,20},{20,12},{12,4},{4,0},{1,9},{9... | collective-permute-start | bytes 786440 | tf_op jit(solution)/shard_map/ppermute | solution.py:299
  33.5 1.6 %collective-permute-start.13 = (bf16[4,128,256]{2,1,0:T(8,128)(2,1)S(1)}, bf16[4,128,256]{2,1,0:T(8,128)(2,1)S(1)}, u32[]{:S(2)}, u32[]{:S(2)}) collective-permute-start(bf16[4,128,256]{2,1,0:T(8,128)(2,1)S(1)} %collective-permute-done.3.refs_3_), channel_id=1, source_target_pairs={{0,8},{8,16},{16,24},{24,28},{28,20},{20,12},{12,4},{4,0},{1,9},{9... | collective-permute-start | bytes 786440 | tf_op jit(solution)/shard_map/ppermute | solution.py:299
  36.3 2.5 %collective-permute-done.8.refs_0_ = bf16[4,128,256]{2,1,0:T(8,128)(2,1)S(1)} collective-permute-done((bf16[4,128,256]{2,1,0:T(8,128)(2,1)S(1)}, bf16[4,128,256]{2,1,0:T(8,128)(2,1)S(1)}, u32[]{:S(2)}, u32[]{:S(2)}) %collective-permute-start.8) | collective-permute-done | bytes 262176 | tf_op jit(solution)/shard_map/ppermute | solution.py:296
  39.0 5.6 %collective-permute-done.11.refs_5_ = bf16[4,128,256]{2,1,0:T(8,128)(2,1)S(1)} collective-permute-done((bf16[4,128,256]{2,1,0:T(8,128)(2,1)S(1)}, bf16[4,128,256]{2,1,0:T(8,128)(2,1)S(1)}, u32[]{:S(2)}, u32[]{:S(2)}) %collective-permute-start.11) | collective-permute-done | bytes 262176 | tf_op jit(solution)/shard_map/ppermute | solution.py:299
  44.6 3.3 %collective-permute-done.13.refs_3_ = bf16[4,128,256]{2,1,0:T(8,128)(2,1)S(1)} collective-permute-done((bf16[4,128,256]{2,1,0:T(8,128)(2,1)S(1)}, bf16[4,128,256]{2,1,0:T(8,128)(2,1)S(1)}, u32[]{:S(2)}, u32[]{:S(2)}) %collective-permute-start.13) | collective-permute-done | bytes 262176 | tf_op jit(solution)/shard_map/ppermute | solution.py:299
  53.4 3.7 %collective-permute-done.14.refs_1_ = bf16[4,128,256]{2,1,0:T(8,128)(2,1)S(1)} collective-permute-done((bf16[4,128,256]{2,1,0:T(8,128)(2,1)S(1)}, bf16[4,128,256]{2,1,0:T(8,128)(2,1)S(1)}, u32[]{:S(2)}, u32[]{:S(2)}) %collective-permute-start.14) | collective-permute-done | bytes 262176 | tf_op jit(solution)/shard_map/ppermute | solution.py:299
  65.9 1.6 %collective-permute-start.23 = (bf16[4,128,256]{2,1,0:T(8,128)(2,1)S(1)}, bf16[4,128,256]{2,1,0:T(8,128)(2,1)S(1)}, u32[]{:S(2)}, u32[]{:S(2)}) collective-permute-start(bf16[4,128,256]{2,1,0:T(8,128)(2,1)S(1)} %collective-permute-done.17.refs_2_), channel_id=1, source_target_pairs={{0,8},{8,16},{16,24},{24,28},{28,20},{20,12},{12,4},{4,0},{1,9},{9... | collective-permute-start | bytes 786440 | tf_op jit(solution)/shard_map/ppermute | solution.py:299
  68.0 1.6 %collective-permute-start.21 = (bf16[256,512]{1,0:T(8,128)(2,1)S(1)}, bf16[256,512]{1,0:T(8,128)(2,1)S(1)}, u32[]{:S(2)}, u32[]{:S(2)}) collective-permute-start(bf16[256,512]{1,0:T(8,128)(2,1)S(1)} %fusion), channel_id=1, source_target_pairs={{0,2},{1,3},{2,0},{3,1},{4,6},{5,7},{6,4},{7,5},{8,10},{9,11},{10,... | collective-permute-start | bytes 786440 | tf_op jit(solution)/shard_map/ppermute | solution.py:357
  70.9 3.7 %collective-permute-done.23.refs_1_ = bf16[4,128,256]{2,1,0:T(8,128)(2,1)S(1)} collective-permute-done((bf16[4,128,256]{2,1,0:T(8,128)(2,1)S(1)}, bf16[4,128,256]{2,1,0:T(8,128)(2,1)S(1)}, u32[]{:S(2)}, u32[]{:S(2)}) %collective-permute-start.23) | collective-permute-done | bytes 262176 | tf_op jit(solution)/shard_map/ppermute | solution.py:299
  75.9 1.6 %collective-permute-start.25 = (bf16[4,128,256]{2,1,0:T(8,128)(2,1)S(1)}, bf16[4,128,256]{2,1,0:T(8,128)(2,1)S(1)}, u32[]{:S(2)}, u32[]{:S(2)}) collective-permute-start(bf16[4,128,256]{2,1,0:T(8,128)(2,1)S(1)} %collective-permute-done.19.refs_3_), channel_id=1, source_target_pairs={{0,8},{8,16},{16,24},{24,28},{28,20},{20,12},{12,4},{4,0},{1,9},{9... | collective-permute-start | bytes 786440 | tf_op jit(solution)/shard_map/ppermute | solution.py:299
  78.1 5.5 %collective-permute-done.25.refs_3_ = bf16[4,128,256]{2,1,0:T(8,128)(2,1)S(1)} collective-permute-done((bf16[4,128,256]{2,1,0:T(8,128)(2,1)S(1)}, bf16[4,128,256]{2,1,0:T(8,128)(2,1)S(1)}, u32[]{:S(2)}, u32[]{:S(2)}) %collective-permute-start.25) | collective-permute-done | bytes 262176 | tf_op jit(solution)/shard_map/ppermute | solution.py:299
  85.5 1.6 %collective-permute-start.28 = (bf16[4,128,256]{2,1,0:T(8,128)(2,1)S(1)}, bf16[4,128,256]{2,1,0:T(8,128)(2,1)S(1)}, u32[]{:S(2)}, u32[]{:S(2)}) collective-permute-start(bf16[4,128,256]{2,1,0:T(8,128)(2,1)S(1)} %collective-permute-done.23.refs_1_), channel_id=1, source_target_pairs={{0,8},{8,16},{16,24},{24,28},{28,20},{20,12},{12,4},{4,0},{1,9},{9... | collective-permute-start | bytes 786440 | tf_op jit(solution)/shard_map/ppermute | solution.py:299
  88.2 1.7 %collective-permute-start.30 = (bf16[4,128,256]{2,1,0:T(8,128)(2,1)S(1)}, bf16[4,128,256]{2,1,0:T(8,128)(2,1)S(1)}, u32[]{:S(2)}, u32[]{:S(2)}) collective-permute-start(bf16[4,128,256]{2,1,0:T(8,128)(2,1)S(1)} %collective-permute-done.25.refs_3_), channel_id=1, source_target_pairs={{0,8},{8,16},{16,24},{24,28},{28,20},{20,12},{12,4},{4,0},{1,9},{9... | collective-permute-start | bytes 786440 | tf_op jit(solution)/shard_map/ppermute | solution.py:299
  90.0 7.9 %orthonormal_first.1 = (f32[256,1024]{1,0:T(8,128)S(1)}, f32[256,256]{1,0:T(8,128)S(1)}) custom-call(s32[10]{0:T(128)S(1)} %pad_add_fusion.2.info, f32[256,512]{1,0:T(8,128)S(1)} %bitcast_subtract_fusion.1.mine, f32[256,512]{1,0:T(8,128)S(1)} %collective-permute-done.26.other), custom_call_target="tpu_custom_call" | custom-call | flops 8589934592 | bytes 2359296 | tf_op jit(solution)/shard_map/orthonormal_first/pallas_call | solution.py:265
  98.5 7.5 %orthonormal_last.1 = (bf16[256,1024]{1,0:T(8,128)(2,1)S(1)}, f32[256,256]{1,0:T(8,128)S(1)}) custom-call(s32[10]{0:T(128)S(1)} %pad_add_fusion.2.info, f32[256,1024]{1,0:T(8,128)S(1)} %get-tuple-element.130.y, f32[256,256]{1,0:T(8,128)S(1)} %get-tuple-element.132.begun), custom_call_target="tpu_custom_call" | custom-call | flops 8589934592 | bytes 2097152 | tf_op jit(solution)/shard_map/orthonormal_last/pallas_call | solution.py:265
  113.6 1.6 %copy-done.1 = bf16[4,1024,256]{2,1,0:T(8,128)(2,1)S(1)} copy-done((bf16[4,1024,256]{2,1,0:T(8,128)(2,1)S(1)}, bf16[4,1024,256]{2,1,0:T(8,128)(2,1)}, u32[]{:S(2)}) %copy-start.1) | copy-done | bytes 2097176
  117.7 1.6 %copy-done.14 = bf16[1,4,1024,256]{3,2,1,0:T(8,128)(2,1)S(1)} copy-done((bf16[1,4,1024,256]{3,2,1,0:T(8,128)(2,1)S(1)}, bf16[1,4,1024,256]{3,2,1,0:T(8,128)(2,1)}, u32[]{:S(2)}) %copy-start.14) | copy-done | bytes 2097176
  121.4 4.2 %project.2 = (bf16[2,256,256]{2,1,0:T(8,128)(2,1)S(1)}, f32[2,256,256]{2,1,0:T(8,128)S(1)}, f32[256,256]{1,0:T(8,128)S(1)}) custom-call(s32[10]{0:T(128)S(1)} %pad_add_fusion.2.info, bf16[256,1024]{1,0:T(8,128)(2,1)S(1)} %copy-done.22, bf16[4,1024,256]{2,1,0:T(8,128)(2,1)S(1)} %bitcast.57, bf16[4,256,256]{2,1,0:T(8,128)(2,1)S(1)} %copy-done.18, ...), custom_call_target="tpu_custom_call" | custom-call | flops 2415919104 | bytes 6291456 | tf_op jit(solution)/shard_map/project/pallas_call | solution.py:265
  129.0 14.8 %orthonormal.1 = (bf16[256,1024]{1,0:T(8,128)(2,1)S(1)}, f32[256,256]{1,0:T(8,128)S(1)}) custom-call(s32[10]{0:T(128)S(1)} %pad_add_fusion.2.info, f32[256,512]{1,0:T(8,128)S(1)} %bitcast_subtract_fusion.mine, f32[256,512]{1,0:T(8,128)S(1)} %collective-permute-done.33.other), custom_call_target="tpu_custom_call" | custom-call | flops 17179869184 | bytes 1835008 | tf_op jit(solution)/shard_map/orthonormal/pallas_call | solution.py:265
  143.8 3.9 %project.3 = (bf16[2,256,256]{2,1,0:T(8,128)(2,1)S(1)}, f32[2,256,256]{2,1,0:T(8,128)S(1)}, f32[256,256]{1,0:T(8,128)S(1)}) custom-call(s32[10]{0:T(128)S(1)} %pad_add_fusion.2.info, bf16[256,1024]{1,0:T(8,128)(2,1)S(1)} %get-tuple-element.174.qt, bf16[4,1024,256]{2,1,0:T(8,128)(2,1)S(1)} %bitcast.58, bf16[4,256,256]{2,1,0:T(8,128)(2,1)S(1)} %copy-done.20, ...), custom_call_target="tpu_custom_call" | custom-call | flops 2415919104 | bytes 6291456 | tf_op jit(solution)/shard_map/project/pallas_call | solution.py:265
  151.1 3.3 %collective-permute-done.35 = bf16[256,256]{1,0:T(8,128)(2,1)S(1)} collective-permute-done((bf16[256,256]{1,0:T(8,128)(2,1)S(1)}, bf16[256,256]{1,0:T(8,128)(2,1)S(1)}, u32[]{:S(2)}, u32[]{:S(2)}) %collective-permute-start.35) | collective-permute-done | bytes 131104 | tf_op jit(solution)/shard_map/ppermute | solution.py:357
  154.5 2.1 %collective-permute-done.37 = bf16[256,256]{1,0:T(8,128)(2,1)S(1)} collective-permute-done((bf16[256,256]{1,0:T(8,128)(2,1)S(1)}, bf16[256,256]{1,0:T(8,128)(2,1)S(1)}, u32[]{:S(2)}, u32[]{:S(2)}) %collective-permute-start.37) | collective-permute-done | bytes 131104 | tf_op jit(solution)/shard_map/ppermute | solution.py:357
  (136 shorter events, 51.1 us)
Async XLA Ops:
  1.8 10.1 %collective-permute-start.5 = (bf16[4,128,256]{2,1,0:T(8,128)(2,1)S(1)}, bf16[4,128,256]{2,1,0:T(8,128)(2,1)S(1)}, u32[]{:S(2)}, u32[]{:S(2)}) collective-permute-start(bf16[4,128,256]{2,1,0:T(8,128)(2,1)S(1)} %get-tuple-element.184.refs_0_), channel_id=1, source_target_pairs={{0,8},{8,16},{16,24},{24,28},{28,20},{20,12},{12,4},{4,0},{1,9},{9... | collective-permute-start | bytes 786440 | tf_op jit(solution)/shard_map/ppermute | solution.py:299
  4.8 9.3 %collective-permute-start.4 = (bf16[4,128,256]{2,1,0:T(8,128)(2,1)S(1)}, bf16[4,128,256]{2,1,0:T(8,128)(2,1)}, u32[]{:S(2)}, u32[]{:S(2)}) collective-permute-start(bf16[4,128,256]{2,1,0:T(8,128)(2,1)S(1)} %get-tuple-element.184.refs_0_), channel_id=1, source_target_pairs={{8,0},{16,8},{24,16},{28,24},{20,28},{12,20},{4,12},{0,4},{9,1},{1... | collective-permute-start | bytes 786440 | tf_op jit(solution)/shard_map/ppermute | solution.py:296
  5.9 11.7 %collective-permute-start.2 = (bf16[4,128,256]{2,1,0:T(8,128)(2,1)S(1)}, bf16[4,128,256]{2,1,0:T(8,128)(2,1)}, u32[]{:S(2)}, u32[]{:S(2)}) collective-permute-start(bf16[4,128,256]{2,1,0:T(8,128)(2,1)S(1)} %get-tuple-element.183.refs_3_), channel_id=1, source_target_pairs={{0,8},{8,16},{16,24},{24,28},{28,20},{20,12},{12,4},{4,0},{1,9},{9... | collective-permute-start | bytes 786440 | tf_op jit(solution)/shard_map/ppermute | solution.py:299
  8.0 11.8 %collective-permute-start = (bf16[4,128,256]{2,1,0:T(8,128)(2,1)S(1)}, bf16[4,128,256]{2,1,0:T(8,128)(2,1)}, u32[]{:S(2)}, u32[]{:S(2)}) collective-permute-start(bf16[4,128,256]{2,1,0:T(8,128)(2,1)S(1)} %get-tuple-element.183.refs_3_), channel_id=1, source_target_pairs={{8,0},{16,8},{24,16},{28,24},{20,28},{12,20},{4,12},{0,4},{9,1},{1... | collective-permute-start | bytes 786440 | tf_op jit(solution)/shard_map/ppermute | solution.py:296
  11.9 17.6 %collective-permute-start.7 = (bf16[4,128,256]{2,1,0:T(8,128)(2,1)S(1)}, bf16[4,128,256]{2,1,0:T(8,128)(2,1)S(1)}, u32[]{:S(2)}, u32[]{:S(2)}) collective-permute-start(bf16[4,128,256]{2,1,0:T(8,128)(2,1)S(1)} %collective-permute-done.5.refs_2_), channel_id=1, source_target_pairs={{0,8},{8,16},{16,24},{24,28},{28,20},{20,12},{12,4},{4,0},{1,9},{9... | collective-permute-start | bytes 786440 | tf_op jit(solution)/shard_map/ppermute | solution.py:299
  14.2 15.3 %collective-permute-start.6 = (bf16[4,128,256]{2,1,0:T(8,128)(2,1)}, bf16[4,128,256]{2,1,0:T(8,128)(2,1)S(1)}, u32[]{:S(2)}, u32[]{:S(2)}) collective-permute-start(bf16[4,128,256]{2,1,0:T(8,128)(2,1)} %collective-permute-done.4.refs_1_), channel_id=1, source_target_pairs={{8,0},{16,8},{24,16},{28,24},{20,28},{12,20},{4,12},{0,4},{9,1},{1... | collective-permute-start | bytes 786440 | tf_op jit(solution)/shard_map/ppermute | solution.py:296
  17.6 10.3 %collective-permute-start.3 = (bf16[4,128,256]{2,1,0:T(8,128)(2,1)}, bf16[4,128,256]{2,1,0:T(8,128)(2,1)S(1)}, u32[]{:S(2)}, u32[]{:S(2)}) collective-permute-start(bf16[4,128,256]{2,1,0:T(8,128)(2,1)} %collective-permute-done.2.refs_5_), channel_id=1, source_target_pairs={{0,8},{8,16},{16,24},{24,28},{28,20},{20,12},{12,4},{4,0},{1,9},{9... | collective-permute-start | bytes 786440 | tf_op jit(solution)/shard_map/ppermute | solution.py:299
  19.8 9.7 %collective-permute-start.1 = (bf16[4,128,256]{2,1,0:T(8,128)(2,1)}, bf16[4,128,256]{2,1,0:T(8,128)(2,1)S(1)}, u32[]{:S(2)}, u32[]{:S(2)}) collective-permute-start(bf16[4,128,256]{2,1,0:T(8,128)(2,1)} %collective-permute-done.refs_4_), channel_id=1, source_target_pairs={{8,0},{16,8},{24,16},{28,24},{20,28},{12,20},{4,12},{0,4},{9,1},{1... | collective-permute-start | bytes 786440 | tf_op jit(solution)/shard_map/ppermute | solution.py:296
  29.5 9.2 %collective-permute-start.8 = (bf16[4,128,256]{2,1,0:T(8,128)(2,1)S(1)}, bf16[4,128,256]{2,1,0:T(8,128)(2,1)S(1)}, u32[]{:S(2)}, u32[]{:S(2)}) collective-permute-start(bf16[4,128,256]{2,1,0:T(8,128)(2,1)S(1)} %collective-permute-done.6.refs_0_), channel_id=1, source_target_pairs={{8,0},{16,8},{24,16},{28,24},{20,28},{12,20},{4,12},{0,4},{9,1},{1... | collective-permute-start | bytes 786440 | tf_op jit(solution)/shard_map/ppermute | solution.py:296
  29.8 9.2 %collective-permute-start.9 = (bf16[4,128,256]{2,1,0:T(8,128)(2,1)S(1)}, bf16[4,128,256]{2,1,0:T(8,128)(2,1)S(1)}, u32[]{:S(2)}, u32[]{:S(2)}) collective-permute-start(bf16[4,128,256]{2,1,0:T(8,128)(2,1)S(1)} %collective-permute-done.7.refs_1_), channel_id=1, source_target_pairs={{0,8},{8,16},{16,24},{24,28},{28,20},{20,12},{12,4},{4,0},{1,9},{9... | collective-permute-start | bytes 786440 | tf_op jit(solution)/shard_map/ppermute | solution.py:299
  31.5 13.1 %collective-permute-start.11 = (bf16[4,128,256]{2,1,0:T(8,128)(2,1)S(1)}, bf16[4,128,256]{2,1,0:T(8,128)(2,1)S(1)}, u32[]{:S(2)}, u32[]{:S(2)}) collective-permute-start(bf16[4,128,256]{2,1,0:T(8,128)(2,1)S(1)} %get-tuple-element.104.refs_3_), channel_id=1, source_target_pairs={{0,8},{8,16},{16,24},{24,28},{28,20},{20,12},{12,4},{4,0},{1,9},{9... | collective-permute-start | bytes 786440 | tf_op jit(solution)/shard_map/ppermute | solution.py:299
  33.1 11.5 %collective-permute-start.10 = (bf16[4,128,256]{2,1,0:T(8,128)(2,1)S(1)}, bf16[4,128,256]{2,1,0:T(8,128)(2,1)S(1)}, u32[]{:S(2)}, u32[]{:S(2)}) collective-permute-start(bf16[4,128,256]{2,1,0:T(8,128)(2,1)S(1)} %get-tuple-element.104.refs_3_), channel_id=1, source_target_pairs={{8,0},{16,8},{24,16},{28,24},{20,28},{12,20},{4,12},{0,4},{9,1},{1... | collective-permute-start | bytes 786440 | tf_op jit(solution)/shard_map/ppermute | solution.py:296
  33.5 14.4 %collective-permute-start.13 = (bf16[4,128,256]{2,1,0:T(8,128)(2,1)S(1)}, bf16[4,128,256]{2,1,0:T(8,128)(2,1)S(1)}, u32[]{:S(2)}, u32[]{:S(2)}) collective-permute-start(bf16[4,128,256]{2,1,0:T(8,128)(2,1)S(1)} %collective-permute-done.3.refs_3_), channel_id=1, source_target_pairs={{0,8},{8,16},{16,24},{24,28},{28,20},{20,12},{12,4},{4,0},{1,9},{9... | collective-permute-start | bytes 786440 | tf_op jit(solution)/shard_map/ppermute | solution.py:299
  38.7 13.2 %collective-permute-start.15 = (bf16[4,128,256]{2,1,0:T(8,128)(2,1)S(1)}, bf16[4,128,256]{2,1,0:T(8,128)(2,1)S(1)}, u32[]{:S(2)}, u32[]{:S(2)}) collective-permute-start(bf16[4,128,256]{2,1,0:T(8,128)(2,1)S(1)} %collective-permute-done.1.refs_2_), channel_id=1, source_target_pairs={{8,0},{16,8},{24,16},{28,24},{20,28},{12,20},{4,12},{0,4},{9,1},{1... | collective-permute-start | bytes 786440 | tf_op jit(solution)/shard_map/ppermute | solution.py:296
  47.9 9.2 %collective-permute-start.14 = (bf16[4,128,256]{2,1,0:T(8,128)(2,1)S(1)}, bf16[4,128,256]{2,1,0:T(8,128)(2,1)S(1)}, u32[]{:S(2)}, u32[]{:S(2)}) collective-permute-start(bf16[4,128,256]{2,1,0:T(8,128)(2,1)S(1)} %collective-permute-done.13.refs_3_), channel_id=1, source_target_pairs={{0,8},{8,16},{16,24},{24,28},{28,20},{20,12},{12,4},{4,0},{1,9},{9... | collective-permute-start | bytes 786440 | tf_op jit(solution)/shard_map/ppermute | solution.py:299
  49.3 10.5 %collective-permute-start.12 = (bf16[4,128,256]{2,1,0:T(8,128)(2,1)S(1)}, bf16[4,128,256]{2,1,0:T(8,128)(2,1)S(1)}, u32[]{:S(2)}, u32[]{:S(2)}) collective-permute-start(bf16[4,128,256]{2,1,0:T(8,128)(2,1)S(1)} %collective-permute-done.8.refs_0_), channel_id=1, source_target_pairs={{8,0},{16,8},{24,16},{28,24},{20,28},{12,20},{4,12},{0,4},{9,1},{1... | collective-permute-start | bytes 786440 | tf_op jit(solution)/shard_map/ppermute | solution.py:296
  49.9 13.8 %collective-permute-start.17 = (bf16[4,128,256]{2,1,0:T(8,128)(2,1)S(1)}, bf16[4,128,256]{2,1,0:T(8,128)(2,1)S(1)}, u32[]{:S(2)}, u32[]{:S(2)}) collective-permute-start(bf16[4,128,256]{2,1,0:T(8,128)(2,1)S(1)} %get-tuple-element.120.refs_0_), channel_id=1, source_target_pairs={{0,8},{8,16},{16,24},{24,28},{28,20},{20,12},{12,4},{4,0},{1,9},{9... | collective-permute-start | bytes 786440 | tf_op jit(solution)/shard_map/ppermute | solution.py:299
  51.4 12.3 %collective-permute-start.16 = (bf16[4,128,256]{2,1,0:T(8,128)(2,1)S(1)}, bf16[4,128,256]{2,1,0:T(8,128)(2,1)S(1)}, u32[]{:S(2)}, u32[]{:S(2)}) collective-permute-start(bf16[4,128,256]{2,1,0:T(8,128)(2,1)S(1)} %get-tuple-element.120.refs_0_), channel_id=1, source_target_pairs={{8,0},{16,8},{24,16},{28,24},{20,28},{12,20},{4,12},{0,4},{9,1},{1... | collective-permute-start | bytes 786440 | tf_op jit(solution)/shard_map/ppermute | solution.py:296
  52.0 13.1 %collective-permute-start.19 = (bf16[4,128,256]{2,1,0:T(8,128)(2,1)S(1)}, bf16[4,128,256]{2,1,0:T(8,128)(2,1)S(1)}, u32[]{:S(2)}, u32[]{:S(2)}) collective-permute-start(bf16[4,128,256]{2,1,0:T(8,128)(2,1)S(1)} %collective-permute-done.11.refs_5_), channel_id=1, source_target_pairs={{0,8},{8,16},{16,24},{24,28},{28,20},{20,12},{12,4},{4,0},{1,9},{9... | collective-permute-start | bytes 786440 | tf_op jit(solution)/shard_map/ppermute | solution.py:299
  57.1 8.8 %collective-permute-start.18 = (bf16[4,128,256]{2,1,0:T(8,128)(2,1)S(1)}, bf16[4,128,256]{2,1,0:T(8,128)(2,1)S(1)}, u32[]{:S(2)}, u32[]{:S(2)}) collective-permute-start(bf16[4,128,256]{2,1,0:T(8,128)(2,1)S(1)} %collective-permute-done.10.refs_4_), channel_id=1, source_target_pairs={{8,0},{16,8},{24,16},{28,24},{20,28},{12,20},{4,12},{0,4},{9,1},{1... | collective-permute-start | bytes 786440 | tf_op jit(solution)/shard_map/ppermute | solution.py:296
  65.9 8.7 %collective-permute-start.23 = (bf16[4,128,256]{2,1,0:T(8,128)(2,1)S(1)}, bf16[4,128,256]{2,1,0:T(8,128)(2,1)S(1)}, u32[]{:S(2)}, u32[]{:S(2)}) collective-permute-start(bf16[4,128,256]{2,1,0:T(8,128)(2,1)S(1)} %collective-permute-done.17.refs_2_), channel_id=1, source_target_pairs={{0,8},{8,16},{16,24},{24,28},{28,20},{20,12},{12,4},{4,0},{1,9},{9... | collective-permute-start | bytes 786440 | tf_op jit(solution)/shard_map/ppermute | solution.py:299
  67.5 8.4 %collective-permute-start.22 = (bf16[4,128,256]{2,1,0:T(8,128)(2,1)S(1)}, bf16[4,128,256]{2,1,0:T(8,128)(2,1)S(1)}, u32[]{:S(2)}, u32[]{:S(2)}) collective-permute-start(bf16[4,128,256]{2,1,0:T(8,128)(2,1)S(1)} %collective-permute-done.16.refs_1_), channel_id=1, source_target_pairs={{8,0},{16,8},{24,16},{28,24},{20,28},{12,20},{4,12},{0,4},{9,1},{1... | collective-permute-start | bytes 786440 | tf_op jit(solution)/shard_map/ppermute | solution.py:296
  68.0 9.9 %collective-permute-start.21 = (bf16[256,512]{1,0:T(8,128)(2,1)S(1)}, bf16[256,512]{1,0:T(8,128)(2,1)S(1)}, u32[]{:S(2)}, u32[]{:S(2)}) collective-permute-start(bf16[256,512]{1,0:T(8,128)(2,1)S(1)} %fusion), channel_id=1, source_target_pairs={{0,2},{1,3},{2,0},{3,1},{4,6},{5,7},{6,4},{7,5},{8,10},{9,11},{10,... | collective-permute-start | bytes 786440 | tf_op jit(solution)/shard_map/ppermute | solution.py:357
  75.9 7.6 %collective-permute-start.25 = (bf16[4,128,256]{2,1,0:T(8,128)(2,1)S(1)}, bf16[4,128,256]{2,1,0:T(8,128)(2,1)S(1)}, u32[]{:S(2)}, u32[]{:S(2)}) collective-permute-start(bf16[4,128,256]{2,1,0:T(8,128)(2,1)S(1)} %collective-permute-done.19.refs_3_), channel_id=1, source_target_pairs={{0,8},{8,16},{16,24},{24,28},{28,20},{20,12},{12,4},{4,0},{1,9},{9... | collective-permute-start | bytes 786440 | tf_op jit(solution)/shard_map/ppermute | solution.py:299
  77.5 7.3 %collective-permute-start.24 = (bf16[4,128,256]{2,1,0:T(8,128)(2,1)S(1)}, bf16[4,128,256]{2,1,0:T(8,128)(2,1)S(1)}, u32[]{:S(2)}, u32[]{:S(2)}) collective-permute-start(bf16[4,128,256]{2,1,0:T(8,128)(2,1)S(1)} %collective-permute-done.18.refs_2_), channel_id=1, source_target_pairs={{8,0},{16,8},{24,16},{28,24},{20,28},{12,20},{4,12},{0,4},{9,1},{1... | collective-permute-start | bytes 786440 | tf_op jit(solution)/shard_map/ppermute | solution.py:296
  85.0 12.9 %collective-permute-start.27 = (bf16[4,128,256]{2,1,0:T(8,128)(2,1)S(1)}, bf16[4,128,256]{2,1,0:T(8,128)(2,1)S(1)}, u32[]{:S(2)}, u32[]{:S(2)}) collective-permute-start(bf16[4,128,256]{2,1,0:T(8,128)(2,1)S(1)} %collective-permute-done.22.refs_0_), channel_id=1, source_target_pairs={{8,0},{16,8},{24,16},{28,24},{20,28},{12,20},{4,12},{0,4},{9,1},{1... | collective-permute-start | bytes 786440 | tf_op jit(solution)/shard_map/ppermute | solution.py:296
  85.5 12.4 %collective-permute-start.28 = (bf16[4,128,256]{2,1,0:T(8,128)(2,1)S(1)}, bf16[4,128,256]{2,1,0:T(8,128)(2,1)S(1)}, u32[]{:S(2)}, u32[]{:S(2)}) collective-permute-start(bf16[4,128,256]{2,1,0:T(8,128)(2,1)S(1)} %collective-permute-done.23.refs_1_), channel_id=1, source_target_pairs={{0,8},{8,16},{16,24},{24,28},{28,20},{20,12},{12,4},{4,0},{1,9},{9... | collective-permute-start | bytes 786440 | tf_op jit(solution)/shard_map/ppermute | solution.py:299
  88.2 18.9 %collective-permute-start.30 = (bf16[4,128,256]{2,1,0:T(8,128)(2,1)S(1)}, bf16[4,128,256]{2,1,0:T(8,128)(2,1)S(1)}, u32[]{:S(2)}, u32[]{:S(2)}) collective-permute-start(bf16[4,128,256]{2,1,0:T(8,128)(2,1)S(1)} %collective-permute-done.25.refs_3_), channel_id=1, source_target_pairs={{0,8},{8,16},{16,24},{24,28},{28,20},{20,12},{12,4},{4,0},{1,9},{9... | collective-permute-start | bytes 786440 | tf_op jit(solution)/shard_map/ppermute | solution.py:299
  97.9 9.2 %collective-permute-start.29 = (bf16[4,128,256]{2,1,0:T(8,128)(2,1)S(1)}, bf16[4,128,256]{2,1,0:T(8,128)(2,1)S(1)}, u32[]{:S(2)}, u32[]{:S(2)}) collective-permute-start(bf16[4,128,256]{2,1,0:T(8,128)(2,1)S(1)} %collective-permute-done.27.refs_0_), channel_id=1, source_target_pairs={{8,0},{16,8},{24,16},{28,24},{20,28},{12,20},{4,12},{0,4},{9,1},{1... | collective-permute-start | bytes 786440 | tf_op jit(solution)/shard_map/ppermute | solution.py:296
  112.1 13.4 %collective-permute-start.32 = (bf16[256,512]{1,0:T(8,128)(2,1)}, bf16[256,512]{1,0:T(8,128)(2,1)}, u32[]{:S(2)}, u32[]{:S(2)}) collective-permute-start(bf16[256,512]{1,0:T(8,128)(2,1)} %fusion.1), channel_id=1, source_target_pairs={{0,2},{1,3},{2,0},{3,1},{4,6},{5,7},{6,4},{7,5},{8,10},{9,11},{10,... | collective-permute-start | bytes 786440 | tf_op jit(solution)/shard_map/ppermute | solution.py:357
  148.1 6.3 %collective-permute-start.35 = (bf16[256,256]{1,0:T(8,128)(2,1)S(1)}, bf16[256,256]{1,0:T(8,128)(2,1)S(1)}, u32[]{:S(2)}, u32[]{:S(2)}) collective-permute-start(bf16[256,256]{1,0:T(8,128)(2,1)S(1)} %fusion.4), channel_id=1, source_target_pairs={{0,2},{1,3},{2,0},{3,1},{4,6},{5,7},{6,4},{7,5},{8,10},{9,11},{10,... | collective-permute-start | bytes 393224 | tf_op jit(solution)/shard_map/ppermute | solution.py:357
  149.6 7.0 %collective-permute-start.37 = (bf16[256,256]{1,0:T(8,128)(2,1)S(1)}, bf16[256,256]{1,0:T(8,128)(2,1)S(1)}, u32[]{:S(2)}, u32[]{:S(2)}) collective-permute-start(bf16[256,256]{1,0:T(8,128)(2,1)S(1)} %fusion.5), channel_id=1, source_target_pairs={{0,2},{1,3},{2,0},{3,1},{4,6},{5,7},{6,4},{7,5},{8,10},{9,11},{10,... | collective-permute-start | bytes 393224 | tf_op jit(solution)/shard_map/ppermute | solution.py:357
  (33 other events, 199.8 us)
